TPU v7x, 256 devices: a whole 4x4x8 slice. The times are simulated.
256 devices in a mesh: ctx: 16 (over z_hi, y, core), head: 16 (over z_lo, x).
Axes of the slice: x: 4, y: 4, z: 8 (z_hi: 2, z_lo: 4; z = z_hi * 4 + z_lo), core: 2. Of those that a mesh axis runs over, the one named last changes fastest.
Arguments:
- query: bfloat16 [7168, 4096], P('ctx', 'head'), may hold values from -80 to 80
- key_states: bfloat16 [7168, 1024], P('ctx'), may hold values from -4 to 4
- value_states: bfloat16 [7168, 1024], P('ctx'), may hold values from -6 to 6
- d_out: bfloat16 [7168, 4096], P('ctx', 'head'), may hold values from -6 to 6
- span_order: int32 [32], P('ctx'), may hold values from 0 to 31, each once
Outputs:
- d_query: bfloat16 [7168, 4096], P('ctx', 'head')
- d_key: bfloat16 [7168, 1024], P('ctx', 'head')
- d_value: bfloat16 [7168, 1024], P('ctx', 'head')
All inputs are finite; a program needn't handle non-finite values.
Results may differ from a plain program's by a relative error of at most 0.007.
Values may be sent and summed in bfloat16 or wider, within the bound.
No kernel may reach another device: no remote copies, remote signals or barrier semaphores. Data moves between devices by JAX's collectives and lax.ppermute only.
A program may use at most 64 MiB of HBM per device.

v0:
```python
import functools
import math

import jax
import jax.numpy as jnp
from jax import lax
from jax.experimental import pallas as pl
from jax.experimental.pallas import tpu as pltpu
from jax.sharding import PartitionSpec as P

HD = 128
CH = 224
ROWS = 2 * CH
PAIR = 2 * ROWS
LANES = 2 * ROWS
TAG = 16
LIMIT = 28
SCALE = HD ** (-0.5)
LOG2_SCALE = SCALE * math.log2(math.e)
HIDDEN = -3e38
LOWEST = -1e30
F32 = jnp.float32
BF16 = jnp.bfloat16
VMEM = pl.BlockSpec(memory_space=pltpu.VMEM)


def turned(block, step):
    route = [(i, i & 9 | ((i >> 1) + step & 3) << 1) for i in range(16)]
    return lax.ppermute(block, "ctx", route)


def core_swapped(block):
    return lax.ppermute(block, "ctx", [(i, i ^ 1) for i in range(16)])


def far_swapped(block):
    return lax.ppermute(block, "ctx", [(i, i ^ 8) for i in range(16)])


def pair_swapped(block):
    return lax.ppermute(block, "head", [(i, i ^ 1) for i in range(16)])


def tagged(span_order, *sides):
    width = sum(side.shape[1] for side in sides)
    tag = jnp.broadcast_to(jnp.pad(span_order.astype(BF16), (0, TAG - 2))[:, None], (TAG, width))
    return jnp.concatenate([jnp.concatenate(sides, axis=1), tag], axis=0)


def dot(a, b, dims):
    return lax.dot_general(a, b, (dims, ((), ())), preferred_element_type=F32)


def tags(ref):
    rows = ref[ROWS : ROWS + TAG, :HD].astype(F32)
    wide = [jnp.concatenate([rows[i : i + 1]] * (LANES // HD), axis=1) for i in range(2)]
    return [w.astype(jnp.int32) * CH for w in wide]


def row_positions(ref):
    low, high = tags(ref)
    lane = lax.broadcasted_iota(jnp.int32, (1, LANES), 1)
    lane = jnp.where(lane >= ROWS, lane - ROWS, lane)
    return jnp.where(lane >= CH, high + lane - CH, low + lane)


def stacked(ref, at):
    return jnp.concatenate([ref[:ROWS, at : at + HD], ref[:ROWS, at + HD : at + 2 * HD]], axis=0)


def pair_of(near, far):
    k = jnp.concatenate([near[:ROWS, :HD], far[:ROWS, :HD]], axis=0)
    v = jnp.concatenate([near[:ROWS, HD:], far[:ROWS, HD:]], axis=0)
    starts = tags(near) + tags(far)
    return k, v, starts


def total_kernel(gather, *refs):
    qo, refs = refs[0], refs[1:]
    if gather:
        blocks, stat, kv = refs[:8], refs[8], refs[9]
        for i, block in enumerate(blocks):
            kv[i] = block[...]
    else:
        kv, earlier, stat = refs
        stat[:8] = earlier[...]
        stat = stat.at[8:16]
    q, o = stacked(qo, 0), stacked(qo, 2 * HD)
    at = row_positions(qo)
    key_row = lax.broadcasted_iota(jnp.int32, (CH, LANES), 0)

    def step(i, state):
        biggest, summed, weighted = state
        k, v, starts = pair_of(kv.at[2 * i], kv.at[2 * i + 1])
        score = dot(k, q, ((1,), (1,)))
        d_prob = dot(v, o, ((1,), (1,)))
        parts = []
        newest = biggest
        for j, start in enumerate(starts):
            part = score[j * CH : (j + 1) * CH] * LOG2_SCALE
            part = jnp.where(key_row <= at - start, part, HIDDEN).reshape(CH // 8, 8, LANES)
            newest = jnp.maximum(newest, jnp.max(part, axis=0))
            parts.append(part)
        factor = jnp.exp2(biggest - newest)
        summed = summed * factor
        weighted = weighted * factor
        for j, part in enumerate(parts):
            expo = jnp.exp2(part - newest[None])
            summed += jnp.sum(expo, axis=0)
            weighted += jnp.sum(expo * d_prob[j * CH : (j + 1) * CH].reshape(CH // 8, 8, LANES), axis=0)
        return newest, summed, weighted

    nothing = jnp.zeros((8, LANES), F32)
    biggest, summed, weighted = lax.fori_loop(0, 4, step, (nothing + LOWEST, nothing, nothing))
    top = jnp.max(biggest, axis=0, keepdims=True)
    factor = jnp.exp2(biggest - top)
    stat[0:1] = top
    stat[1:2] = jnp.sum(summed * factor, axis=0, keepdims=True)
    stat[2:3] = jnp.sum(weighted * factor, axis=0, keepdims=True)
    stat[3:8] = jnp.zeros((5, LANES), F32)


def call(kernel, name, outs, *operands):
    return pl.pallas_call(
        kernel,
        out_shape=[jax.ShapeDtypeStruct(*out) for out in outs],
        in_specs=[VMEM] * len(operands),
        out_specs=[VMEM] * len(outs),
        compiler_params=pltpu.CompilerParams(vmem_limit_bytes=LIMIT << 20),
        cost_estimate=pl.CostEstimate(flops=1 << 20, bytes_accessed=1 << 16, transcendentals=0),
        name=name,
    )(*operands)


def merged(here, there):
    top = jnp.maximum(here[0:1], there[0:1])
    mine, other = jnp.exp2(here[0:1] - top), jnp.exp2(there[0:1] - top)
    summed = here[1:2] * mine + there[1:2] * other
    weighted = here[2:3] * mine + there[2:3] * other
    return top + jnp.log2(summed), weighted / summed


def rows_of(qo, here, there):
    return stacked(qo, 0), stacked(qo, 2 * HD), row_positions(qo), *merged(here, there)


def tile(rows, near, far):
    q, o, at, lse, delta = rows
    k, v, starts = pair_of(near, far)
    key_row = lax.broadcasted_iota(jnp.int32, (CH, LANES), 0)
    score = dot(k, q, ((1,), (1,)))
    d_prob = dot(v, o, ((1,), (1,)))
    probs, d_scores = [], []
    for j, start in enumerate(starts):
        here = slice(j * CH, (j + 1) * CH)
        prob = jnp.exp2(score[here] * LOG2_SCALE - lse)
        prob = jnp.where(key_row <= at - start, prob, 0.0)
        d_scores.append((prob * (d_prob[here] - delta)).astype(BF16))
        probs.append(prob.astype(BF16))
    d_score = jnp.concatenate(d_scores, axis=0)
    prob = jnp.concatenate(probs, axis=0)
    return (
        dot(d_score, q, ((1,), (0,))) * SCALE,
        dot(prob, o, ((1,), (0,))),
        dot(k, d_score, ((0,), (0,))) * SCALE,
    )


def split_pair(term_k, term_v, own_part, far_part):
    own_part[:, :HD] = term_k[:ROWS]
    own_part[:, HD:] = term_v[:ROWS]
    far_part[:, :HD] = term_k[ROWS:].astype(BF16)
    far_part[:, HD:] = term_v[ROWS:].astype(BF16)


def put_rows(out, dq):
    rows = dq.T
    out[:, :HD] = rows[:ROWS].astype(out.dtype)
    out[:, HD:] = rows[ROWS:].astype(out.dtype)


def pair_kernel(place, qo, qo_far, stats, stats_far, kv, *refs):
    own_part, far_part, dq, dq_far = refs[-4:]
    old, old_far = refs[:2] if len(refs) > 4 else (None, None)
    near, far = kv.at[2 * place], kv.at[2 * place + 1]
    far_k, far_v, far_q = tile(rows_of(qo_far, stats[8:16], stats_far[0:8]), near, far)
    dq_far[...] = far_q if old is None else old_far[...] + far_q
    term_k, term_v, term_q = tile(rows_of(qo, stats[0:8], stats_far[8:16]), near, far)
    dq[...] = term_q if old is None else old[...] + term_q
    split_pair(term_k + far_k, term_v + far_v, own_part, far_part)


def far_kernel(qo_far, stats, stats_far, kv, dq, out, terms):
    term_k, term_v, term_q = tile(rows_of(qo_far, stats[8:16], stats_far[0:8]), kv.at[0], kv.at[1])
    put_rows(out, dq[...] + term_q)
    terms[:, :HD] = term_k
    terms[:, HD:] = term_v


def last_kernel(qo, stats, stats_far, kv, dq, terms, own_part, far_part, out):
    term_k, term_v, term_q = tile(rows_of(qo, stats[0:8], stats_far[8:16]), kv.at[0], kv.at[1])
    put_rows(out, dq[...] + term_q)
    split_pair(term_k + terms[:, :HD], term_v + terms[:, HD:], own_part, far_part)


def finish_kernel(dq, dq_far, kept, incoming, d_query, d_key, d_value):
    d_query[...] = (dq[...] + dq_far[...].astype(F32)).astype(BF16)
    both = (kept[...] + incoming[...].astype(F32)).T
    d_key[...] = both[: HD // 2].astype(BF16)
    d_value[...] = both[HD // 2 :].astype(BF16)


def on_device(query, key_states, value_states, d_out, span_order):
    head_index = lax.axis_index("head")
    first = head_index // 2 * HD
    k_own = lax.dynamic_slice_in_dim(key_states, first, HD, 1)
    v_own = lax.dynamic_slice_in_dim(value_states, first, HD, 1)
    kv = tagged(span_order, k_own, v_own)
    qo = tagged(span_order, query, d_out)
    qo_far = far_swapped(qo)
    near = [kv, turned(kv, 1), turned(kv, 3), turned(kv, 2)]
    far = [core_swapped(block) for block in near]
    blocks = [b for pair in zip(near, far) for b in pair]
    gathered = ((8, ROWS + TAG, 2 * HD), BF16)
    here, kv = call(functools.partial(total_kernel, True), "totals", [((8, LANES), F32), gathered], qo, *blocks)
    qo_far, kv = lax.optimization_barrier((qo_far, kv))
    (stats,) = call(functools.partial(total_kernel, False), "totals", [((16, LANES), F32)], qo_far, kv, here)
    stats_far = far_swapped(stats)
    halves = [((ROWS, 2 * HD), F32), ((ROWS, 2 * HD), BF16)]
    transposed = [((HD, LANES), F32)] * 2

    def grads(place, *before):
        kernel = functools.partial(pair_kernel, place)
        return call(kernel, "grads", halves + transposed, qo, qo_far, stats, stats_far, kv, *before)

    def joined(own_part, far_part):
        return (own_part + core_swapped(far_part).astype(F32)).astype(BF16)

    *part_a, dq, dq_far = grads(3)
    *part_b, dq, dq_far = grads(2, dq, dq_far)
    *part_c, dq, dq_far = grads(1, dq, dq_far)
    part_a = joined(*part_a)
    dq_far, part_a = lax.optimization_barrier((dq_far, part_a))
    part_a = turned(part_a, 2)
    far_outs = [((ROWS, 2 * HD), BF16), ((PAIR, 2 * HD), F32)]
    dq_far, terms = call(far_kernel, "far", far_outs, qo_far, stats, stats_far, kv, dq_far)
    part_b = joined(*part_b)
    dq, part_b, terms = lax.optimization_barrier((dq, part_b, terms))
    part_b = turned(part_b, 1)
    own_part, far_part, dq = call(last_kernel, "last", halves + halves[:1], qo, stats, stats_far, kv, dq, terms)
    arrived = [part_a, part_b, turned(joined(*part_c), 3)]
    dq_far = far_swapped(dq_far)
    grad = own_part + core_swapped(far_part).astype(F32)
    for part in arrived:
        grad = grad + part.astype(F32)
    half = HD // 2
    keep_at = head_index % 2 * half
    give_at = half - keep_at

    def cut(at):
        return jnp.concatenate([lax.dynamic_slice_in_dim(grad, first + at, half, 1) for first in (0, HD)], axis=1)

    incoming = pair_swapped(cut(give_at).astype(BF16))
    outs = [((ROWS, 2 * HD), BF16)] + [((half, ROWS), BF16)] * 2
    d_query, d_key, d_value = call(finish_kernel, "finish", outs, dq, dq_far, cut(keep_at), incoming)
    return d_query, d_key.T, d_value.T


def solution(mesh):
    return jax.shard_map(
        on_device,
        mesh=mesh,
        in_specs=(P("ctx", "head"), P("ctx", None), P("ctx", None), P("ctx", "head"), P("ctx")),
        out_specs=(P("ctx", "head"), P("ctx", "head"), P("ctx", "head")),
        check_vma=False,
    )
```

profile of v0, /device:TPU:34, one launch (start us, length us, event | category | flops | bytes accessed | tf_op | source)
XLA Modules:
  0.0 92.8 jit_solution(10291544921727097609)
XLA Ops:
  1.4 1.0 %constant_dynamic-slice_fusion.2 = (bf16[448,128]{1,0:T(8,128)(2,1)S(1)}, bf16[448,128]{1,0:T(8,128)(2,1)S(1)}) fusion(bf16[448,1024]{1,0:T(8,128)(2,1)} %param.7, s32[]{:T(128)S(6)} %select_n.28, bf16[448,1024]{1,0:T(8,128)(2,1)} %param.6), kind=kLoop, calls=%fused_computation.12 | loop fusion | bytes 458756 | tf_op jit(solution)/shard_map/dynamic_slice | solution.py:217
  2.5 3.3 %collective-permute-start.6 = (bf16[464,256]{1,0:T(8,128)(2,1)S(1)}, bf16[464,256]{1,0:T(8,128)(2,1)S(1)}, u32[]{:S(2)}, u32[]{:S(2)}) collective-permute-start(bf16[464,256]{1,0:T(8,128)(2,1)S(1)} %maximum_maximum_fusion.1.refs_1_), channel_id=1, source_target_pairs={{0,64},{16,80},{32,96},{48,112},{64,0},{80,16},{96,32},{112,48},{1... | collective-permute-start | bytes 712712 | tf_op jit(solution)/shard_map/ppermute | solution.py:29
  5.8 1.1 %collective-permute-start.4 = (bf16[464,256]{1,0:T(8,128)(2,1)S(1)}, bf16[464,256]{1,0:T(8,128)(2,1)S(1)}, u32[]{:S(2)}, u32[]{:S(2)}) collective-permute-start(bf16[464,256]{1,0:T(8,128)(2,1)S(1)} %maximum_maximum_fusion.1.refs_1_), channel_id=1, source_target_pairs={{0,96},{16,112},{32,0},{48,16},{64,32},{80,48},{96,64},{112,80},{1... | collective-permute-start | bytes 712712 | tf_op jit(solution)/shard_map/ppermute | solution.py:29
  6.8 1.0 %collective-permute-start.2 = (bf16[464,256]{1,0:T(8,128)(2,1)S(1)}, bf16[464,256]{1,0:T(8,128)(2,1)S(1)}, u32[]{:S(2)}, u32[]{:S(2)}) collective-permute-start(bf16[464,256]{1,0:T(8,128)(2,1)S(1)} %maximum_maximum_fusion.1.refs_1_), channel_id=1, source_target_pairs={{0,32},{16,48},{32,64},{48,80},{64,96},{80,112},{96,0},{112,16},{1... | collective-permute-start | bytes 712712 | tf_op jit(solution)/shard_map/ppermute | solution.py:29
  7.8 1.2 %maximum_maximum_fusion.refs_0_.qo = bf16[464,512]{1,0:T(8,128)(2,1)S(1)} fusion(bf16[448,256]{1,0:T(8,128)(2,1)} %param.8, bf16[448,256]{1,0:T(8,128)(2,1)} %param.5, bf16[464]{0:T(512)(128)(2,1)S(1)} %pad.15.clone), kind=kLoop, calls=%fused_computation | loop fusion | flops 1425408 | bytes 934816 | tf_op jit(solution)/shard_map/concatenate | solution.py:47
  9.0 6.4 %collective-permute-start = (bf16[464,512]{1,0:T(8,128)(2,1)S(1)}, bf16[464,512]{1,0:T(8,128)(2,1)S(1)}, u32[]{:S(2)}, u32[]{:S(2)}) collective-permute-start(bf16[464,512]{1,0:T(8,128)(2,1)S(1)} %maximum_maximum_fusion.refs_0_.qo), channel_id=1, source_target_pairs={{0,128},{16,144},{32,160},{48,176},{64,192},{80,208},{96,224},{112... | collective-permute-start | bytes 1425416 | tf_op jit(solution)/shard_map/ppermute | solution.py:37
  15.9 1.2 %collective-permute-done.4.refs_5_ = bf16[464,256]{1,0:T(8,128)(2,1)S(1)} collective-permute-done((bf16[464,256]{1,0:T(8,128)(2,1)S(1)}, bf16[464,256]{1,0:T(8,128)(2,1)S(1)}, u32[]{:S(2)}, u32[]{:S(2)}) %collective-permute-start.4) | collective-permute-done | bytes 237600 | tf_op jit(solution)/shard_map/ppermute | solution.py:29
  17.6 1.0 %collective-permute-done.5.refs_6_ = bf16[464,256]{1,0:T(8,128)(2,1)S(1)} collective-permute-done((bf16[464,256]{1,0:T(8,128)(2,1)S(1)}, bf16[464,256]{1,0:T(8,128)(2,1)S(1)}, u32[]{:S(2)}, u32[]{:S(2)}) %collective-permute-start.5) | collective-permute-done | bytes 237600 | tf_op jit(solution)/shard_map/ppermute | solution.py:33
  18.9 5.4 %totals.2 = (f32[8,896]{1,0:T(8,128)S(1)}, bf16[8,464,256]{2,1,0:T(8,128)(2,1)S(1)}) custom-call(bf16[464,512]{1,0:T(8,128)(2,1)S(1)} %maximum_maximum_fusion.refs_0_.qo, bf16[464,256]{1,0:T(8,128)(2,1)S(1)} %maximum_maximum_fusion.1.refs_1_, bf16[464,256]{1,0:T(8,128)(2,1)S(1)} %collective-permute-done.1.refs_2_, ...), custom_call_target="tpu_custom_call" | custom-call | flops 1048576 | bytes 65536 | tf_op jit(solution)/shard_map/totals/pallas_call | solution.py:124
  24.3 11.4 %collective-permute-done.refs_0_.qo_far = bf16[464,512]{1,0:T(8,128)(2,1)S(1)} collective-permute-done((bf16[464,512]{1,0:T(8,128)(2,1)S(1)}, bf16[464,512]{1,0:T(8,128)(2,1)S(1)}, u32[]{:S(2)}, u32[]{:S(2)}) %collective-permute-start) | collective-permute-done | bytes 475168 | tf_op jit(solution)/shard_map/ppermute | solution.py:37
  35.7 5.3 %totals.3.stats = f32[16,896]{1,0:T(8,128)S(1)} custom-call(bf16[464,512]{1,0:T(8,128)(2,1)S(1)} %collective-permute-done.refs_0_.qo_far, bf16[8,464,256]{2,1,0:T(8,128)(2,1)S(1)} %get-tuple-element.34.refs_1_.kv, f32[8,896]{1,0:T(8,128)S(1)} %get-tuple-element.35.refs_2_), custom_call_target="tpu_custom_call" | custom-call | flops 1048576 | bytes 65536 | tf_op jit(solution)/shard_map/totals/pallas_call | solution.py:124
  41.0 5.8 %collective-permute-start.8 = (f32[16,896]{1,0:T(8,128)S(1)}, f32[16,896]{1,0:T(8,128)S(1)}, u32[]{:S(2)}, u32[]{:S(2)}) collective-permute-start(f32[16,896]{1,0:T(8,128)S(1)} %totals.3.stats), channel_id=1, source_target_pairs={{0,128},{16,144},{32,160},{48,176},{64,192},{80,208},{96,224},{112... | collective-permute-start | bytes 172040 | tf_op jit(solution)/shard_map/ppermute | solution.py:37
  46.8 2.5 %collective-permute-done.8.stats_far = f32[16,896]{1,0:T(8,128)S(1)} collective-permute-done((f32[16,896]{1,0:T(8,128)S(1)}, f32[16,896]{1,0:T(8,128)S(1)}, u32[]{:S(2)}, u32[]{:S(2)}) %collective-permute-start.8) | collective-permute-done | bytes 57376 | tf_op jit(solution)/shard_map/ppermute | solution.py:37
  49.3 5.2 %grads.3 = (f32[448,256]{1,0:T(8,128)S(1)}, bf16[448,256]{1,0:T(8,128)(2,1)S(1)}, f32[128,896]{1,0:T(8,128)S(1)}, f32[128,896]{1,0:T(8,128)S(1)}) custom-call(bf16[464,512]{1,0:T(8,128)(2,1)S(1)} %maximum_maximum_fusion.refs_0_.qo, bf16[464,512]{1,0:T(8,128)(2,1)S(1)} %collective-permute-done.refs_0_.qo_far, f32[16,896]{1,0:T(8,128)S(1)} %totals.3.stats, ...), custom_call_target="tpu_custom_call" | custom-call | flops 1048576 | bytes 65536 | tf_op jit(solution)/shard_map/grads/pallas_call | solution.py:124
  54.6 5.2 %grads.4 = (f32[448,256]{1,0:T(8,128)S(1)}, bf16[448,256]{1,0:T(8,128)(2,1)S(1)}, f32[128,896]{1,0:T(8,128)S(1)}, f32[128,896]{1,0:T(8,128)S(1)}) custom-call(bf16[464,512]{1,0:T(8,128)(2,1)S(1)} %maximum_maximum_fusion.refs_0_.qo, bf16[464,512]{1,0:T(8,128)(2,1)S(1)} %collective-permute-done.refs_0_.qo_far, f32[16,896]{1,0:T(8,128)S(1)} %totals.3.stats, ...), custom_call_target="tpu_custom_call" | custom-call | flops 1048576 | bytes 65536 | tf_op jit(solution)/shard_map/grads/pallas_call | solution.py:124
  60.6 5.2 %grads.5 = (f32[448,256]{1,0:T(8,128)S(1)}, bf16[448,256]{1,0:T(8,128)(2,1)S(1)}, f32[128,896]{1,0:T(8,128)S(1)}, f32[128,896]{1,0:T(8,128)S(1)}) custom-call(bf16[464,512]{1,0:T(8,128)(2,1)S(1)} %maximum_maximum_fusion.refs_0_.qo, bf16[464,512]{1,0:T(8,128)(2,1)S(1)} %collective-permute-done.refs_0_.qo_far, f32[16,896]{1,0:T(8,128)S(1)} %totals.3.stats, ...), custom_call_target="tpu_custom_call" | custom-call | flops 1048576 | bytes 65536 | tf_op jit(solution)/shard_map/grads/pallas_call | solution.py:124
  66.0 2.4 %far.1 = (bf16[448,256]{1,0:T(8,128)(2,1)S(1)}, f32[896,256]{1,0:T(8,128)S(1)}) custom-call(bf16[464,512]{1,0:T(8,128)(2,1)S(1)} %collective-permute-done.refs_0_.qo_far, f32[16,896]{1,0:T(8,128)S(1)} %totals.3.stats, f32[16,896]{1,0:T(8,128)S(1)} %collective-permute-done.8.stats_far, bf16[8,464,256]{2,1,0:T(8,128)(2,1)S(1)} %get-tuple-element.34.refs_1_.kv, ...), custom_call_target="tpu_custom_call" | custom-call | flops 1048576 | bytes 65536 | tf_op jit(solution)/shard_map/far/pallas_call | solution.py:124
  68.5 3.0 %last.1 = (f32[448,256]{1,0:T(8,128)S(1)}, bf16[448,256]{1,0:T(8,128)(2,1)S(1)}, f32[448,256]{1,0:T(8,128)S(1)}) custom-call(bf16[464,512]{1,0:T(8,128)(2,1)S(1)} %maximum_maximum_fusion.refs_0_.qo, f32[16,896]{1,0:T(8,128)S(1)} %totals.3.stats, f32[16,896]{1,0:T(8,128)S(1)} %collective-permute-done.8.stats_far, ...), custom_call_target="tpu_custom_call" | custom-call | flops 1048576 | bytes 65536 | tf_op jit(solution)/shard_map/last/pallas_call | solution.py:124
  72.7 3.1 %collective-permute-start.13 = (bf16[448,256]{1,0:T(8,128)(2,1)S(1)}, bf16[448,256]{1,0:T(8,128)(2,1)S(1)}, u32[]{:S(2)}, u32[]{:S(2)}) collective-permute-start(bf16[448,256]{1,0:T(8,128)(2,1)S(1)} %add_convert_fusion.1), channel_id=1, source_target_pairs={{0,64},{16,80},{32,96},{48,112},{64,0},{80,16},{96,32},{112,48},{1... | collective-permute-start | bytes 688136 | tf_op jit(solution)/shard_map/ppermute | solution.py:29
  75.9 5.6 %collective-permute-start.11 = (bf16[448,256]{1,0:T(8,128)(2,1)S(1)}, bf16[448,256]{1,0:T(8,128)(2,1)S(1)}, u32[]{:S(2)}, u32[]{:S(2)}) collective-permute-start(bf16[448,256]{1,0:T(8,128)(2,1)S(1)} %get-tuple-element.51), channel_id=1, source_target_pairs={{0,128},{16,144},{32,160},{48,176},{64,192},{80,208},{96,224},{112... | collective-permute-start | bytes 688136 | tf_op jit(solution)/shard_map/ppermute | solution.py:37
  81.6 4.9 %collective-permute-done.13 = bf16[448,256]{1,0:T(8,128)(2,1)S(1)} collective-permute-done((bf16[448,256]{1,0:T(8,128)(2,1)S(1)}, bf16[448,256]{1,0:T(8,128)(2,1)S(1)}, u32[]{:S(2)}, u32[]{:S(2)}) %collective-permute-start.13) | collective-permute-done | bytes 229408 | tf_op jit(solution)/shard_map/ppermute | solution.py:29
  88.0 2.3 %collective-permute-done.11.dq_far = bf16[448,256]{1,0:T(8,128)(2,1)S(1)} collective-permute-done((bf16[448,256]{1,0:T(8,128)(2,1)S(1)}, bf16[448,256]{1,0:T(8,128)(2,1)S(1)}, u32[]{:S(2)}, u32[]{:S(2)}) %collective-permute-start.11) | collective-permute-done | bytes 229408 | tf_op jit(solution)/shard_map/ppermute | solution.py:37
  90.2 1.7 %collective-permute-done.17.incoming = bf16[448,128]{1,0:T(8,128)(2,1)S(1)} collective-permute-done((bf16[448,128]{1,0:T(8,128)(2,1)S(1)}, bf16[448,128]{1,0:T(8,128)(2,1)S(1)}, u32[]{:S(2)}, u32[]{:S(2)}) %collective-permute-start.17) | collective-permute-done | bytes 114720 | tf_op jit(solution)/shard_map/ppermute | solution.py:41
  91.9 0.9 finish.1
  (34 shorter events, 6.2 us)
Async XLA Ops:
  2.5 12.9 %collective-permute-start.6 = (bf16[464,256]{1,0:T(8,128)(2,1)S(1)}, bf16[464,256]{1,0:T(8,128)(2,1)S(1)}, u32[]{:S(2)}, u32[]{:S(2)}) collective-permute-start(bf16[464,256]{1,0:T(8,128)(2,1)S(1)} %maximum_maximum_fusion.1.refs_1_), channel_id=1, source_target_pairs={{0,64},{16,80},{32,96},{48,112},{64,0},{80,16},{96,32},{112,48},{1... | collective-permute-start | bytes 712712 | tf_op jit(solution)/shard_map/ppermute | solution.py:29
  5.8 11.3 %collective-permute-start.4 = (bf16[464,256]{1,0:T(8,128)(2,1)S(1)}, bf16[464,256]{1,0:T(8,128)(2,1)S(1)}, u32[]{:S(2)}, u32[]{:S(2)}) collective-permute-start(bf16[464,256]{1,0:T(8,128)(2,1)S(1)} %maximum_maximum_fusion.1.refs_1_), channel_id=1, source_target_pairs={{0,96},{16,112},{32,0},{48,16},{64,32},{80,48},{96,64},{112,80},{1... | collective-permute-start | bytes 712712 | tf_op jit(solution)/shard_map/ppermute | solution.py:29
  6.8 10.3 %collective-permute-start.2 = (bf16[464,256]{1,0:T(8,128)(2,1)S(1)}, bf16[464,256]{1,0:T(8,128)(2,1)S(1)}, u32[]{:S(2)}, u32[]{:S(2)}) collective-permute-start(bf16[464,256]{1,0:T(8,128)(2,1)S(1)} %maximum_maximum_fusion.1.refs_1_), channel_id=1, source_target_pairs={{0,32},{16,48},{32,64},{48,80},{64,96},{80,112},{96,0},{112,16},{1... | collective-permute-start | bytes 712712 | tf_op jit(solution)/shard_map/ppermute | solution.py:29
  9.0 26.7 %collective-permute-start = (bf16[464,512]{1,0:T(8,128)(2,1)S(1)}, bf16[464,512]{1,0:T(8,128)(2,1)S(1)}, u32[]{:S(2)}, u32[]{:S(2)}) collective-permute-start(bf16[464,512]{1,0:T(8,128)(2,1)S(1)} %maximum_maximum_fusion.refs_0_.qo), channel_id=1, source_target_pairs={{0,128},{16,144},{32,160},{48,176},{64,192},{80,208},{96,224},{112... | collective-permute-start | bytes 1425416 | tf_op jit(solution)/shard_map/ppermute | solution.py:37
  15.4 2.2 %collective-permute-start.1 = (bf16[464,256]{1,0:T(8,128)(2,1)S(1)}, bf16[464,256]{1,0:T(8,128)(2,1)S(1)}, u32[]{:S(2)}, u32[]{:S(2)}) collective-permute-start(bf16[464,256]{1,0:T(8,128)(2,1)S(1)} %maximum_maximum_fusion.1.refs_1_), channel_id=1, source_target_pairs={{0,16},{16,0},{32,48},{48,32},{64,80},{80,64},{96,112},{112,96},{1... | collective-permute-start | bytes 712712 | tf_op jit(solution)/shard_map/ppermute | solution.py:33
  15.4 2.2 %collective-permute-start.7 = (bf16[464,256]{1,0:T(8,128)(2,1)S(1)}, bf16[464,256]{1,0:T(8,128)(2,1)S(1)}, u32[]{:S(2)}, u32[]{:S(2)}) collective-permute-start(bf16[464,256]{1,0:T(8,128)(2,1)S(1)} %collective-permute-done.6.refs_7_), channel_id=1, source_target_pairs={{0,16},{16,0},{32,48},{48,32},{64,80},{80,64},{96,112},{112,96},{1... | collective-permute-start | bytes 712712 | tf_op jit(solution)/shard_map/ppermute | solution.py:33
  17.1 1.5 %collective-permute-start.5 = (bf16[464,256]{1,0:T(8,128)(2,1)S(1)}, bf16[464,256]{1,0:T(8,128)(2,1)S(1)}, u32[]{:S(2)}, u32[]{:S(2)}) collective-permute-start(bf16[464,256]{1,0:T(8,128)(2,1)S(1)} %collective-permute-done.4.refs_5_), channel_id=1, source_target_pairs={{0,16},{16,0},{32,48},{48,32},{64,80},{80,64},{96,112},{112,96},{1... | collective-permute-start | bytes 712712 | tf_op jit(solution)/shard_map/ppermute | solution.py:33
  17.1 1.8 %collective-permute-start.3 = (bf16[464,256]{1,0:T(8,128)(2,1)S(1)}, bf16[464,256]{1,0:T(8,128)(2,1)S(1)}, u32[]{:S(2)}, u32[]{:S(2)}) collective-permute-start(bf16[464,256]{1,0:T(8,128)(2,1)S(1)} %collective-permute-done.2.refs_3_), channel_id=1, source_target_pairs={{0,16},{16,0},{32,48},{48,32},{64,80},{80,64},{96,112},{112,96},{1... | collective-permute-start | bytes 712712 | tf_op jit(solution)/shard_map/ppermute | solution.py:33
  41.0 8.4 %collective-permute-start.8 = (f32[16,896]{1,0:T(8,128)S(1)}, f32[16,896]{1,0:T(8,128)S(1)}, u32[]{:S(2)}, u32[]{:S(2)}) collective-permute-start(f32[16,896]{1,0:T(8,128)S(1)} %totals.3.stats), channel_id=1, source_target_pairs={{0,128},{16,144},{32,160},{48,176},{64,192},{80,208},{96,224},{112... | collective-permute-start | bytes 172040 | tf_op jit(solution)/shard_map/ppermute | solution.py:37
  54.5 11.4 %collective-permute-start.10 = (bf16[448,256]{1,0:T(8,128)(2,1)S(1)}, bf16[448,256]{1,0:T(8,128)(2,1)S(1)}, u32[]{:S(2)}, u32[]{:S(2)}) collective-permute-start(bf16[448,256]{1,0:T(8,128)(2,1)S(1)} %get-tuple-element.45), channel_id=1, source_target_pairs={{0,16},{16,0},{32,48},{48,32},{64,80},{80,64},{96,112},{112,96},{1... | collective-permute-start | bytes 688136 | tf_op jit(solution)/shard_map/ppermute | solution.py:33
  59.8 8.6 %collective-permute-start.9 = (bf16[448,256]{1,0:T(8,128)(2,1)S(1)}, bf16[448,256]{1,0:T(8,128)(2,1)S(1)}, u32[]{:S(2)}, u32[]{:S(2)}) collective-permute-start(bf16[448,256]{1,0:T(8,128)(2,1)S(1)} %get-tuple-element.42), channel_id=1, source_target_pairs={{0,16},{16,0},{32,48},{48,32},{64,80},{80,64},{96,112},{112,96},{1... | collective-permute-start | bytes 688136 | tf_op jit(solution)/shard_map/ppermute | solution.py:33
  65.8 9.9 %collective-permute-start.15 = (bf16[448,256]{1,0:T(8,128)(2,1)S(1)}, bf16[448,256]{1,0:T(8,128)(2,1)S(1)}, u32[]{:S(2)}, u32[]{:S(2)}) collective-permute-start(bf16[448,256]{1,0:T(8,128)(2,1)S(1)} %get-tuple-element.57), channel_id=1, source_target_pairs={{0,16},{16,0},{32,48},{48,32},{64,80},{80,64},{96,112},{112,96},{1... | collective-permute-start | bytes 688136 | tf_op jit(solution)/shard_map/ppermute | solution.py:33
  71.5 10.1 %collective-permute-start.12 = (bf16[448,256]{1,0:T(8,128)(2,1)S(1)}, bf16[448,256]{1,0:T(8,128)(2,1)S(1)}, u32[]{:S(2)}, u32[]{:S(2)}) collective-permute-start(bf16[448,256]{1,0:T(8,128)(2,1)S(1)} %get-tuple-element.53), channel_id=1, source_target_pairs={{0,16},{16,0},{32,48},{48,32},{64,80},{80,64},{96,112},{112,96},{1... | collective-permute-start | bytes 688136 | tf_op jit(solution)/shard_map/ppermute | solution.py:33
  72.0 9.6 %collective-permute-start.14 = (bf16[448,256]{1,0:T(8,128)(2,1)S(1)}, bf16[448,256]{1,0:T(8,128)(2,1)S(1)}, u32[]{:S(2)}, u32[]{:S(2)}) collective-permute-start(bf16[448,256]{1,0:T(8,128)(2,1)S(1)} %add_convert_fusion.2), channel_id=1, source_target_pairs={{0,32},{16,48},{32,64},{48,80},{64,96},{80,112},{96,0},{112,16},{1... | collective-permute-start | bytes 688136 | tf_op jit(solution)/shard_map/ppermute | solution.py:29
  72.7 13.8 %collective-permute-start.13 = (bf16[448,256]{1,0:T(8,128)(2,1)S(1)}, bf16[448,256]{1,0:T(8,128)(2,1)S(1)}, u32[]{:S(2)}, u32[]{:S(2)}) collective-permute-start(bf16[448,256]{1,0:T(8,128)(2,1)S(1)} %add_convert_fusion.1), channel_id=1, source_target_pairs={{0,64},{16,80},{32,96},{48,112},{64,0},{80,16},{96,32},{112,48},{1... | collective-permute-start | bytes 688136 | tf_op jit(solution)/shard_map/ppermute | solution.py:29
  75.8 10.8 %collective-permute-start.16 = (bf16[448,256]{1,0:T(8,128)(2,1)S(1)}, bf16[448,256]{1,0:T(8,128)(2,1)S(1)}, u32[]{:S(2)}, u32[]{:S(2)}) collective-permute-start(bf16[448,256]{1,0:T(8,128)(2,1)S(1)} %add_convert_fusion), channel_id=1, source_target_pairs={{0,96},{16,112},{32,0},{48,16},{64,32},{80,48},{96,64},{112,80},{1... | collective-permute-start | bytes 688136 | tf_op jit(solution)/shard_map/ppermute | solution.py:29
  75.9 14.3 %collective-permute-start.11 = (bf16[448,256]{1,0:T(8,128)(2,1)S(1)}, bf16[448,256]{1,0:T(8,128)(2,1)S(1)}, u32[]{:S(2)}, u32[]{:S(2)}) collective-permute-start(bf16[448,256]{1,0:T(8,128)(2,1)S(1)} %get-tuple-element.51), channel_id=1, source_target_pairs={{0,128},{16,144},{32,160},{48,176},{64,192},{80,208},{96,224},{112... | collective-permute-start | bytes 688136 | tf_op jit(solution)/shard_map/ppermute | solution.py:37
  87.0 4.9 %collective-permute-start.17 = (bf16[448,128]{1,0:T(8,128)(2,1)S(1)}, bf16[448,128]{1,0:T(8,128)(2,1)S(1)}, u32[]{:S(2)}, u32[]{:S(2)}) collective-permute-start(bf16[448,128]{1,0:T(8,128)(2,1)S(1)} %pad_maximum_fusion.1), channel_id=1, source_target_pairs={{0,1},{1,0},{2,3},{3,2},{4,5},{5,4},{6,7},{7,6},{8,9},{9,8},{10,11... | collective-permute-start | bytes 344072 | tf_op jit(solution)/shard_map/ppermute | solution.py:41
where the time goes:
time: 93 us; the launch traced here: 92.8 us
  Pallas kernels  32.5 us (35%)
  starting transfers between devices  30.2 us (32%)
  waiting for transfers between devices  25.4 us (27%)
  other arithmetic  2.52 us (3%)
  local copies, waits for them, and re-layouts  1.38 us (1%)
    pallas_call x8, Pallas kernels, call(): pl.pallas_call(kernel, out_shape=[jax.ShapeDtypeStruct(*out) for out in o...  32.5 us
    ppermute x3, starting transfers between devices, far_swapped(): return lax.ppermute(block, 'ctx', [(i, i ^ 8) for i in range(16)])  17.8 us
    ppermute x3, waiting for transfers between devices, far_swapped(): return lax.ppermute(block, 'ctx', [(i, i ^ 8) for i in range(16)])  16.2 us
    ppermute x6, starting transfers between devices, turned(): return lax.ppermute(block, 'ctx', route)  9.12 us
    ppermute x6, waiting for transfers between devices, turned(): return lax.ppermute(block, 'ctx', route)  6.24 us
    ppermute x8, starting transfers between devices, core_swapped(): return lax.ppermute(block, 'ctx', [(i, i ^ 1) for i in range(16)])  2.59 us
  transfers between devices with their start and end apart: 18, of which 9 were waited for; matrix products, arithmetic and copies ran while one was open for 2% of the time, Pallas kernels for 23%

commit v1 on v0

--- a/solution.py
+++ b/solution.py
@@ -82,9 +82,7 @@
         for i, block in enumerate(blocks):
             kv[i] = block[...]
     else:
-        kv, earlier, stat = refs
-        stat[:8] = earlier[...]
-        stat = stat.at[8:16]
+        kv, stat = refs
     q, o = stacked(qo, 0), stacked(qo, 2 * HD)
     at = row_positions(qo)
     key_row = lax.broadcasted_iota(jnp.int32, (CH, LANES), 0)
@@ -179,28 +177,36 @@
     out[:, HD:] = rows[ROWS:].astype(out.dtype)
 
 
-def pair_kernel(place, qo, qo_far, stats, stats_far, kv, *refs):
-    own_part, far_part, dq, dq_far = refs[-4:]
-    old, old_far = refs[:2] if len(refs) > 4 else (None, None)
-    near, far = kv.at[2 * place], kv.at[2 * place + 1]
-    far_k, far_v, far_q = tile(rows_of(qo_far, stats[8:16], stats_far[0:8]), near, far)
-    dq_far[...] = far_q if old is None else old_far[...] + far_q
-    term_k, term_v, term_q = tile(rows_of(qo, stats[0:8], stats_far[8:16]), near, far)
-    dq[...] = term_q if old is None else old[...] + term_q
-    split_pair(term_k + far_k, term_v + far_v, own_part, far_part)
-
-
-def far_kernel(qo_far, stats, stats_far, kv, dq, out, terms):
-    term_k, term_v, term_q = tile(rows_of(qo_far, stats[8:16], stats_far[0:8]), kv.at[0], kv.at[1])
-    put_rows(out, dq[...] + term_q)
-    terms[:, :HD] = term_k
-    terms[:, HD:] = term_v
-
-
-def last_kernel(qo, stats, stats_far, kv, dq, terms, own_part, far_part, out):
-    term_k, term_v, term_q = tile(rows_of(qo, stats[0:8], stats_far[8:16]), kv.at[0], kv.at[1])
-    put_rows(out, dq[...] + term_q)
-    split_pair(term_k + terms[:, :HD], term_v + terms[:, HD:], own_part, far_part)
+def far_kernel(places, qo_far, here, there, kv, *refs):
+    old, refs = (refs[0], refs[1:]) if len(refs) > 3 else (None, refs)
+    out, *terms = refs
+    rows = rows_of(qo_far, here, there)
+    total = None if old is None else old[...]
+    for place, wide in zip(places, terms):
+        term_k, term_v, term_q = tile(rows, kv.at[2 * place], kv.at[2 * place + 1])
+        wide[:, :HD] = term_k
+        wide[:, HD:] = term_v
+        total = term_q if total is None else total + term_q
+    if places[-1] == 0:
+        put_rows(out, total)
+    else:
+        out[...] = total
+
+
+def own_kernel(places, qo, here, there, kv, *refs):
+    terms, refs = refs[: len(places)], refs[len(places) :]
+    own_part, far_part, out = refs[-3:]
+    rows = rows_of(qo, here, there)
+    total = refs[0][...] if len(refs) > 3 else None
+    for i, (place, wide) in enumerate(zip(places, terms)):
+        term_k, term_v, term_q = tile(rows, kv.at[2 * place], kv.at[2 * place + 1])
+        total = term_q if total is None else total + term_q
+        at = pl.ds(i * ROWS, ROWS)
+        split_pair(term_k + wide[:, :HD], term_v + wide[:, HD:], own_part.at[at], far_part.at[at])
+    if places[-1] == 0:
+        put_rows(out, total)
+    else:
+        out[...] = total
 
 
 def finish_kernel(dq, dq_far, kept, incoming, d_query, d_key, d_value):
@@ -222,34 +228,39 @@
     far = [core_swapped(block) for block in near]
     blocks = [b for pair in zip(near, far) for b in pair]
     gathered = ((8, ROWS + TAG, 2 * HD), BF16)
-    here, kv = call(functools.partial(total_kernel, True), "totals", [((8, LANES), F32), gathered], qo, *blocks)
-    qo_far, kv = lax.optimization_barrier((qo_far, kv))
-    (stats,) = call(functools.partial(total_kernel, False), "totals", [((16, LANES), F32)], qo_far, kv, here)
-    stats_far = far_swapped(stats)
+    stat = ((8, LANES), F32)
+    here, kv = call(functools.partial(total_kernel, True), "totals", [stat, gathered], qo, *blocks)
+    here_far = far_swapped(here)
+    qo_far, kv, here = lax.optimization_barrier((qo_far, kv, here))
+    (there,) = call(functools.partial(total_kernel, False), "totals", [stat], qo_far, kv)
+    there_far = far_swapped(there)
     halves = [((ROWS, 2 * HD), F32), ((ROWS, 2 * HD), BF16)]
-    transposed = [((HD, LANES), F32)] * 2
-
-    def grads(place, *before):
-        kernel = functools.partial(pair_kernel, place)
-        return call(kernel, "grads", halves + transposed, qo, qo_far, stats, stats_far, kv, *before)
+    wides, transposed = [((PAIR, 2 * HD), F32)] * 2, [((HD, LANES), F32)]
+
+    def far_grads(places, *before):
+        outs = (halves[1:] if places[-1] == 0 else transposed) + wides
+        return call(functools.partial(far_kernel, places), "far", outs, qo_far, there, here_far, kv, *before)
+
+    def own_grads(places, *before):
+        count = len(places) * ROWS
+        outs = [((count, 2 * HD), F32), ((count, 2 * HD), BF16)] + (halves[:1] if places[-1] == 0 else transposed)
+        return call(functools.partial(own_kernel, places), "own", outs, qo, here, there_far, kv, *before)
 
     def joined(own_part, far_part):
         return (own_part + core_swapped(far_part).astype(F32)).astype(BF16)
 
-    *part_a, dq, dq_far = grads(3)
-    *part_b, dq, dq_far = grads(2, dq, dq_far)
-    *part_c, dq, dq_far = grads(1, dq, dq_far)
-    part_a = joined(*part_a)
-    dq_far, part_a = lax.optimization_barrier((dq_far, part_a))
-    part_a = turned(part_a, 2)
-    far_outs = [((ROWS, 2 * HD), BF16), ((PAIR, 2 * HD), F32)]
-    dq_far, terms = call(far_kernel, "far", far_outs, qo_far, stats, stats_far, kv, dq_far)
-    part_b = joined(*part_b)
-    dq, part_b, terms = lax.optimization_barrier((dq, part_b, terms))
-    part_b = turned(part_b, 1)
-    own_part, far_part, dq = call(last_kernel, "last", halves + halves[:1], qo, stats, stats_far, kv, dq, terms)
-    arrived = [part_a, part_b, turned(joined(*part_c), 3)]
-    dq_far = far_swapped(dq_far)
+    dq_far, *terms = far_grads((3, 2))
+    *parts, dq = own_grads((3, 2), *terms)
+    dq_far, *terms = far_grads((1, 0), dq_far)
+    parts = joined(*parts)
+    part_a, part_b = parts[:ROWS], parts[ROWS:]
+    arrived = [turned(part_a, 2), turned(part_b, 1)]
+    dq_there = far_swapped(dq_far)
+    dq, part_a, part_b, dq_far = lax.optimization_barrier((dq, part_a, part_b, dq_far))
+    *parts, dq = own_grads((1,), terms[0], dq)
+    own_part, far_part, dq = own_grads((0,), terms[1], dq)
+    arrived.append(turned(joined(*parts), 3))
+    *arrived, dq_there = lax.optimization_barrier((*arrived, dq_there))
     grad = own_part + core_swapped(far_part).astype(F32)
     for part in arrived:
         grad = grad + part.astype(F32)
@@ -262,7 +273,7 @@
 
     incoming = pair_swapped(cut(give_at).astype(BF16))
     outs = [((ROWS, 2 * HD), BF16)] + [((half, ROWS), BF16)] * 2
-    d_query, d_key, d_value = call(finish_kernel, "finish", outs, dq, dq_far, cut(keep_at), incoming)
+    d_query, d_key, d_value = call(finish_kernel, "finish", outs, dq, dq_there, cut(keep_at), incoming)
     return d_query, d_key.T, d_value.T
 
 

time: 93 us -> 89.6 us (0.963)
  waiting for transfers between devices: 25.4 us -> 18.2 us
  starting transfers between devices: 30.2 us -> 34.5 us
    ppermute x3 -> x4, waiting for transfers between devices: 16.2 us -> 8.66 us  [far_swapped(): return lax.ppermute(block, 'ctx', [(i, i ^ 8) for i in range(16)])]
    ppermute x3 -> x4, starting transfers between devices: 17.8 us -> 21.7 us  [far_swapped(): return lax.ppermute(block, 'ctx', [(i, i ^ 8) for i in range(16)])]
    ppermute x1, waiting for transfers between devices: 1.68 us -> 4.22 us  [pair_swapped(): return lax.ppermute(block, 'head', [(i, i ^ 1) for i in range(16)])]
    ppermute x6, waiting for transfers between devices: 6.24 us -> 3.81 us  [turned(): return lax.ppermute(block, 'ctx', route)]
    ppermute x6, starting transfers between devices: 9.12 us -> 10.6 us  [turned(): return lax.ppermute(block, 'ctx', route)]
    ppermute x8 -> x7, starting transfers between devices: 2.59 us -> 1.6 us  [core_swapped(): return lax.ppermute(block, 'ctx', [(i, i ^ 1) for i in range(16)])]
  transfers between devices with their start and end apart: 18 -> 18, of which waited for: 9 -> 6; matrix products, arithmetic and copies ran while one was open for 2% -> 2% of each run, Pallas kernels for 23% -> 26%
where the time goes in v1:
time: 89.6 us; the launch traced here: 89.5 us
  starting transfers between devices  34.5 us (39%)
  Pallas kernels  32.1 us (36%)
  waiting for transfers between devices  18.2 us (20%)
  other arithmetic  2.55 us (3%)
  local copies, waits for them, and re-layouts  1.41 us (2%)
    pallas_call x8, Pallas kernels, call(): pl.pallas_call(kernel, out_shape=[jax.ShapeDtypeStruct(*out) for out in o...  32.1 us
    ppermute x4, starting transfers between devices, far_swapped(): return lax.ppermute(block, 'ctx', [(i, i ^ 8) for i in range(16)])  21.7 us
    ppermute x6, starting transfers between devices, turned(): return lax.ppermute(block, 'ctx', route)  10.6 us
    ppermute x4, waiting for transfers between devices, far_swapped(): return lax.ppermute(block, 'ctx', [(i, i ^ 8) for i in range(16)])  8.66 us
    ppermute x1, waiting for transfers between devices, pair_swapped(): return lax.ppermute(block, 'head', [(i, i ^ 1) for i in range(16)])  4.22 us
    ppermute x6, waiting for transfers between devices, turned(): return lax.ppermute(block, 'ctx', route)  3.81 us
  transfers between devices with their start and end apart: 18, of which 6 were waited for; matrix products, arithmetic and copies ran while one was open for 2% of the time, Pallas kernels for 26%

profile of v1, /device:TPU:34, one launch (start us, length us, event | category | flops | bytes accessed | tf_op | source)
XLA Modules:
  0.0 89.5 jit_solution(13126378371015223643)
XLA Ops:
  1.4 1.0 %constant_dynamic-slice_fusion.2 = (bf16[448,128]{1,0:T(8,128)(2,1)S(1)}, bf16[448,128]{1,0:T(8,128)(2,1)S(1)}) fusion(bf16[448,1024]{1,0:T(8,128)(2,1)} %param.7, s32[]{:T(128)S(6)} %select_n.28, bf16[448,1024]{1,0:T(8,128)(2,1)} %param.6), kind=kLoop, calls=%fused_computation.11 | loop fusion | bytes 458756 | tf_op jit(solution)/shard_map/dynamic_slice | solution.py:223
  2.5 1.7 %collective-permute-start.2 = (bf16[464,256]{1,0:T(8,128)(2,1)S(1)}, bf16[464,256]{1,0:T(8,128)(2,1)S(1)}, u32[]{:S(2)}, u32[]{:S(2)}) collective-permute-start(bf16[464,256]{1,0:T(8,128)(2,1)S(1)} %maximum_maximum_fusion.1.refs_1_), channel_id=1, source_target_pairs={{0,32},{16,48},{32,64},{48,80},{64,96},{80,112},{96,0},{112,16},{1... | collective-permute-start | bytes 712712 | tf_op jit(solution)/shard_map/ppermute | solution.py:29
  4.2 1.7 %collective-permute-start.4 = (bf16[464,256]{1,0:T(8,128)(2,1)S(1)}, bf16[464,256]{1,0:T(8,128)(2,1)S(1)}, u32[]{:S(2)}, u32[]{:S(2)}) collective-permute-start(bf16[464,256]{1,0:T(8,128)(2,1)S(1)} %maximum_maximum_fusion.1.refs_1_), channel_id=1, source_target_pairs={{0,96},{16,112},{32,0},{48,16},{64,32},{80,48},{96,64},{112,80},{1... | collective-permute-start | bytes 712712 | tf_op jit(solution)/shard_map/ppermute | solution.py:29
  5.8 2.0 %collective-permute-start.6 = (bf16[464,256]{1,0:T(8,128)(2,1)S(1)}, bf16[464,256]{1,0:T(8,128)(2,1)S(1)}, u32[]{:S(2)}, u32[]{:S(2)}) collective-permute-start(bf16[464,256]{1,0:T(8,128)(2,1)S(1)} %maximum_maximum_fusion.1.refs_1_), channel_id=1, source_target_pairs={{0,64},{16,80},{32,96},{48,112},{64,0},{80,16},{96,32},{112,48},{1... | collective-permute-start | bytes 712712 | tf_op jit(solution)/shard_map/ppermute | solution.py:29
  7.8 1.2 %maximum_maximum_fusion.refs_0_.qo = bf16[464,512]{1,0:T(8,128)(2,1)S(1)} fusion(bf16[448,256]{1,0:T(8,128)(2,1)} %param.8, bf16[448,256]{1,0:T(8,128)(2,1)} %param.5, bf16[464]{0:T(512)(128)(2,1)S(1)} %pad.15.clone), kind=kLoop, calls=%fused_computation.1 | loop fusion | flops 1425408 | bytes 934816 | tf_op jit(solution)/shard_map/concatenate | solution.py:47
  9.0 6.4 %collective-permute-start = (bf16[464,512]{1,0:T(8,128)(2,1)S(1)}, bf16[464,512]{1,0:T(8,128)(2,1)S(1)}, u32[]{:S(2)}, u32[]{:S(2)}) collective-permute-start(bf16[464,512]{1,0:T(8,128)(2,1)S(1)} %maximum_maximum_fusion.refs_0_.qo), channel_id=1, source_target_pairs={{0,128},{16,144},{32,160},{48,176},{64,192},{80,208},{96,224},{112... | collective-permute-start | bytes 1425416 | tf_op jit(solution)/shard_map/ppermute | solution.py:37
  16.0 1.6 %collective-permute-done.6.refs_7_ = bf16[464,256]{1,0:T(8,128)(2,1)S(1)} collective-permute-done((bf16[464,256]{1,0:T(8,128)(2,1)S(1)}, bf16[464,256]{1,0:T(8,128)(2,1)S(1)}, u32[]{:S(2)}, u32[]{:S(2)}) %collective-permute-start.6) | collective-permute-done | bytes 237600 | tf_op jit(solution)/shard_map/ppermute | solution.py:29
  17.7 1.5 %collective-permute-done.7.refs_8_ = bf16[464,256]{1,0:T(8,128)(2,1)S(1)} collective-permute-done((bf16[464,256]{1,0:T(8,128)(2,1)S(1)}, bf16[464,256]{1,0:T(8,128)(2,1)S(1)}, u32[]{:S(2)}, u32[]{:S(2)}) %collective-permute-start.7) | collective-permute-done | bytes 237600 | tf_op jit(solution)/shard_map/ppermute | solution.py:33
  19.1 5.5 %totals.2 = (f32[8,896]{1,0:T(8,128)S(1)}, bf16[8,464,256]{2,1,0:T(8,128)(2,1)S(1)}) custom-call(bf16[464,512]{1,0:T(8,128)(2,1)S(1)} %maximum_maximum_fusion.refs_0_.qo, bf16[464,256]{1,0:T(8,128)(2,1)S(1)} %maximum_maximum_fusion.1.refs_1_, bf16[464,256]{1,0:T(8,128)(2,1)S(1)} %collective-permute-done.1.refs_2_, ...), custom_call_target="tpu_custom_call" | custom-call | flops 1048576 | bytes 65536 | tf_op jit(solution)/shard_map/totals/pallas_call | solution.py:122
  24.7 6.4 %collective-permute-start.9 = (f32[8,896]{1,0:T(8,128)S(1)}, f32[8,896]{1,0:T(8,128)S(1)}, u32[]{:S(2)}, u32[]{:S(2)}) collective-permute-start(f32[8,896]{1,0:T(8,128)S(1)} %get-tuple-element.33.here), channel_id=1, source_target_pairs={{0,128},{16,144},{32,160},{48,176},{64,192},{80,208},{96,224},{112... | collective-permute-start | bytes 86024 | tf_op jit(solution)/shard_map/ppermute | solution.py:37
  31.1 5.5 %collective-permute-done.refs_0_.qo_far = bf16[464,512]{1,0:T(8,128)(2,1)S(1)} collective-permute-done((bf16[464,512]{1,0:T(8,128)(2,1)S(1)}, bf16[464,512]{1,0:T(8,128)(2,1)S(1)}, u32[]{:S(2)}, u32[]{:S(2)}) %collective-permute-start) | collective-permute-done | bytes 475168 | tf_op jit(solution)/shard_map/ppermute | solution.py:37
  36.6 5.4 %totals.3.here = f32[8,896]{1,0:T(8,128)S(1)} custom-call(bf16[464,512]{1,0:T(8,128)(2,1)S(1)} %collective-permute-done.refs_0_.qo_far, bf16[8,464,256]{2,1,0:T(8,128)(2,1)S(1)} %get-tuple-element.35.refs_1_.kv), custom_call_target="tpu_custom_call" | custom-call | flops 1048576 | bytes 65536 | tf_op jit(solution)/shard_map/totals/pallas_call | solution.py:122
  42.0 5.8 %collective-permute-start.8 = (f32[8,896]{1,0:T(8,128)S(1)}, f32[8,896]{1,0:T(8,128)S(1)}, u32[]{:S(2)}, u32[]{:S(2)}) collective-permute-start(f32[8,896]{1,0:T(8,128)S(1)} %totals.3.here), channel_id=1, source_target_pairs={{0,128},{16,144},{32,160},{48,176},{64,192},{80,208},{96,224},{112... | collective-permute-start | bytes 86024 | tf_op jit(solution)/shard_map/ppermute | solution.py:37
  47.8 4.6 %far.2 = (f32[128,896]{1,0:T(8,128)S(1)}, f32[896,256]{1,0:T(8,128)S(1)}, f32[896,256]{1,0:T(8,128)S(1)}) custom-call(bf16[464,512]{1,0:T(8,128)(2,1)S(1)} %collective-permute-done.refs_0_.qo_far, f32[8,896]{1,0:T(8,128)S(1)} %totals.3.here, f32[8,896]{1,0:T(8,128)S(1)} %collective-permute-done.9.there, bf16[8,464,256]{2,1,0:T(8,128)(2,1)S(1)} %get-tuple-element.35.refs_1_.kv), custom_call_target="tpu_custom_call" | custom-call | flops 1048576 | bytes 65536 | tf_op jit(solution)/shard_map/far/pallas_call | solution.py:122
  52.5 5.0 %own.3 = (f32[896,256]{1,0:T(8,128)S(1)}, bf16[896,256]{1,0:T(8,128)(2,1)S(1)}, f32[128,896]{1,0:T(8,128)S(1)}) custom-call(bf16[464,512]{1,0:T(8,128)(2,1)S(1)} %maximum_maximum_fusion.refs_0_.qo, f32[8,896]{1,0:T(8,128)S(1)} %get-tuple-element.33.here, f32[8,896]{1,0:T(8,128)S(1)} %collective-permute-done.8.there, ...), custom_call_target="tpu_custom_call" | custom-call | flops 1048576 | bytes 65536 | tf_op jit(solution)/shard_map/own/pallas_call | solution.py:122
  57.8 4.7 %far.3 = (bf16[448,256]{1,0:T(8,128)(2,1)S(1)}, f32[896,256]{1,0:T(8,128)S(1)}, f32[896,256]{1,0:T(8,128)S(1)}) custom-call(bf16[464,512]{1,0:T(8,128)(2,1)S(1)} %collective-permute-done.refs_0_.qo_far, f32[8,896]{1,0:T(8,128)S(1)} %totals.3.here, f32[8,896]{1,0:T(8,128)S(1)} %collective-permute-done.9.there, ...), custom_call_target="tpu_custom_call" | custom-call | flops 1048576 | bytes 65536 | tf_op jit(solution)/shard_map/far/pallas_call | solution.py:122
  62.6 3.0 %own.4 = (f32[448,256]{1,0:T(8,128)S(1)}, bf16[448,256]{1,0:T(8,128)(2,1)S(1)}, f32[128,896]{1,0:T(8,128)S(1)}) custom-call(bf16[464,512]{1,0:T(8,128)(2,1)S(1)} %maximum_maximum_fusion.refs_0_.qo, f32[8,896]{1,0:T(8,128)S(1)} %get-tuple-element.33.here, f32[8,896]{1,0:T(8,128)S(1)} %collective-permute-done.8.there, ...), custom_call_target="tpu_custom_call" | custom-call | flops 1048576 | bytes 65536 | tf_op jit(solution)/shard_map/own/pallas_call | solution.py:122
  66.2 3.1 %collective-permute-start.15 = (bf16[448,256]{1,0:T(8,128)(2,1)S(1)}, bf16[448,256]{1,0:T(8,128)(2,1)S(1)}, u32[]{:S(2)}, u32[]{:S(2)}) collective-permute-start(bf16[448,256]{1,0:T(8,128)(2,1)S(1)} %get-tuple-element.44), channel_id=1, source_target_pairs={{0,128},{16,144},{32,160},{48,176},{64,192},{80,208},{96,224},{112... | collective-permute-start | bytes 688136 | tf_op jit(solution)/shard_map/ppermute | solution.py:37
  69.3 1.7 %collective-permute-start.11 = (bf16[448,256]{1,0:T(8,128)(2,1)S(1)}, bf16[448,256]{1,0:T(8,128)(2,1)S(1)}, u32[]{:S(2)}, u32[]{:S(2)}) collective-permute-start(bf16[448,256]{1,0:T(8,128)(2,1)S(1)} %get-tuple-element.64), channel_id=1, source_target_pairs={{0,64},{16,80},{32,96},{48,112},{64,0},{80,16},{96,32},{112,48},{1... | collective-permute-start | bytes 688136 | tf_op jit(solution)/shard_map/ppermute | solution.py:29
  71.1 3.6 %collective-permute-start.14 = (bf16[448,256]{1,0:T(8,128)(2,1)S(1)}, bf16[448,256]{1,0:T(8,128)(2,1)S(1)}, u32[]{:S(2)}, u32[]{:S(2)}) collective-permute-start(bf16[448,256]{1,0:T(8,128)(2,1)S(1)} %add_convert_fusion.1), channel_id=1, source_target_pairs={{0,96},{16,112},{32,0},{48,16},{64,32},{80,48},{96,64},{112,80},{1... | collective-permute-start | bytes 688136 | tf_op jit(solution)/shard_map/ppermute | solution.py:29
  74.7 3.0 %own.5 = (f32[448,256]{1,0:T(8,128)S(1)}, bf16[448,256]{1,0:T(8,128)(2,1)S(1)}, f32[448,256]{1,0:T(8,128)S(1)}) custom-call(bf16[464,512]{1,0:T(8,128)(2,1)S(1)} %maximum_maximum_fusion.refs_0_.qo, f32[8,896]{1,0:T(8,128)S(1)} %get-tuple-element.33.here, f32[8,896]{1,0:T(8,128)S(1)} %collective-permute-done.8.there, ...), custom_call_target="tpu_custom_call" | custom-call | flops 1048576 | bytes 65536 | tf_op jit(solution)/shard_map/own/pallas_call | solution.py:122
  77.8 3.1 %collective-permute-done.15.dq_far = bf16[448,256]{1,0:T(8,128)(2,1)S(1)} collective-permute-done((bf16[448,256]{1,0:T(8,128)(2,1)S(1)}, bf16[448,256]{1,0:T(8,128)(2,1)S(1)}, u32[]{:S(2)}, u32[]{:S(2)}) %collective-permute-start.15) | collective-permute-done | bytes 229408 | tf_op jit(solution)/shard_map/ppermute | solution.py:37
  80.9 2.2 %collective-permute-done.12 = bf16[448,256]{1,0:T(8,128)(2,1)S(1)} collective-permute-done((bf16[448,256]{1,0:T(8,128)(2,1)S(1)}, bf16[448,256]{1,0:T(8,128)(2,1)S(1)}, u32[]{:S(2)}, u32[]{:S(2)}) %collective-permute-start.12) | collective-permute-done | bytes 229408 | tf_op jit(solution)/shard_map/ppermute | solution.py:29
  84.4 4.2 %collective-permute-done.17.incoming = bf16[448,128]{1,0:T(8,128)(2,1)S(1)} collective-permute-done((bf16[448,128]{1,0:T(8,128)(2,1)S(1)}, bf16[448,128]{1,0:T(8,128)(2,1)S(1)}, u32[]{:S(2)}, u32[]{:S(2)}) %collective-permute-start.17) | collective-permute-done | bytes 114720 | tf_op jit(solution)/shard_map/ppermute | solution.py:41
  (34 shorter events, 4.9 us)
Async XLA Ops:
  2.5 12.9 %collective-permute-start.2 = (bf16[464,256]{1,0:T(8,128)(2,1)S(1)}, bf16[464,256]{1,0:T(8,128)(2,1)S(1)}, u32[]{:S(2)}, u32[]{:S(2)}) collective-permute-start(bf16[464,256]{1,0:T(8,128)(2,1)S(1)} %maximum_maximum_fusion.1.refs_1_), channel_id=1, source_target_pairs={{0,32},{16,48},{32,64},{48,80},{64,96},{80,112},{96,0},{112,16},{1... | collective-permute-start | bytes 712712 | tf_op jit(solution)/shard_map/ppermute | solution.py:29
  4.2 11.7 %collective-permute-start.4 = (bf16[464,256]{1,0:T(8,128)(2,1)S(1)}, bf16[464,256]{1,0:T(8,128)(2,1)S(1)}, u32[]{:S(2)}, u32[]{:S(2)}) collective-permute-start(bf16[464,256]{1,0:T(8,128)(2,1)S(1)} %maximum_maximum_fusion.1.refs_1_), channel_id=1, source_target_pairs={{0,96},{16,112},{32,0},{48,16},{64,32},{80,48},{96,64},{112,80},{1... | collective-permute-start | bytes 712712 | tf_op jit(solution)/shard_map/ppermute | solution.py:29
  5.8 11.8 %collective-permute-start.6 = (bf16[464,256]{1,0:T(8,128)(2,1)S(1)}, bf16[464,256]{1,0:T(8,128)(2,1)S(1)}, u32[]{:S(2)}, u32[]{:S(2)}) collective-permute-start(bf16[464,256]{1,0:T(8,128)(2,1)S(1)} %maximum_maximum_fusion.1.refs_1_), channel_id=1, source_target_pairs={{0,64},{16,80},{32,96},{48,112},{64,0},{80,16},{96,32},{112,48},{1... | collective-permute-start | bytes 712712 | tf_op jit(solution)/shard_map/ppermute | solution.py:29
  9.0 27.6 %collective-permute-start = (bf16[464,512]{1,0:T(8,128)(2,1)S(1)}, bf16[464,512]{1,0:T(8,128)(2,1)S(1)}, u32[]{:S(2)}, u32[]{:S(2)}) collective-permute-start(bf16[464,512]{1,0:T(8,128)(2,1)S(1)} %maximum_maximum_fusion.refs_0_.qo), channel_id=1, source_target_pairs={{0,128},{16,144},{32,160},{48,176},{64,192},{80,208},{96,224},{112... | collective-permute-start | bytes 1425416 | tf_op jit(solution)/shard_map/ppermute | solution.py:37
  15.4 2.3 %collective-permute-start.1 = (bf16[464,256]{1,0:T(8,128)(2,1)S(1)}, bf16[464,256]{1,0:T(8,128)(2,1)S(1)}, u32[]{:S(2)}, u32[]{:S(2)}) collective-permute-start(bf16[464,256]{1,0:T(8,128)(2,1)S(1)} %maximum_maximum_fusion.1.refs_1_), channel_id=1, source_target_pairs={{0,16},{16,0},{32,48},{48,32},{64,80},{80,64},{96,112},{112,96},{1... | collective-permute-start | bytes 712712 | tf_op jit(solution)/shard_map/ppermute | solution.py:33
  15.4 2.3 %collective-permute-start.3 = (bf16[464,256]{1,0:T(8,128)(2,1)S(1)}, bf16[464,256]{1,0:T(8,128)(2,1)S(1)}, u32[]{:S(2)}, u32[]{:S(2)}) collective-permute-start(bf16[464,256]{1,0:T(8,128)(2,1)S(1)} %collective-permute-done.2.refs_3_), channel_id=1, source_target_pairs={{0,16},{16,0},{32,48},{48,32},{64,80},{80,64},{96,112},{112,96},{1... | collective-permute-start | bytes 712712 | tf_op jit(solution)/shard_map/ppermute | solution.py:33
  15.9 1.8 %collective-permute-start.5 = (bf16[464,256]{1,0:T(8,128)(2,1)S(1)}, bf16[464,256]{1,0:T(8,128)(2,1)S(1)}, u32[]{:S(2)}, u32[]{:S(2)}) collective-permute-start(bf16[464,256]{1,0:T(8,128)(2,1)S(1)} %collective-permute-done.4.refs_5_), channel_id=1, source_target_pairs={{0,16},{16,0},{32,48},{48,32},{64,80},{80,64},{96,112},{112,96},{1... | collective-permute-start | bytes 712712 | tf_op jit(solution)/shard_map/ppermute | solution.py:33
  17.6 1.5 %collective-permute-start.7 = (bf16[464,256]{1,0:T(8,128)(2,1)S(1)}, bf16[464,256]{1,0:T(8,128)(2,1)S(1)}, u32[]{:S(2)}, u32[]{:S(2)}) collective-permute-start(bf16[464,256]{1,0:T(8,128)(2,1)S(1)} %collective-permute-done.6.refs_7_), channel_id=1, source_target_pairs={{0,16},{16,0},{32,48},{48,32},{64,80},{80,64},{96,112},{112,96},{1... | collective-permute-start | bytes 712712 | tf_op jit(solution)/shard_map/ppermute | solution.py:33
  24.7 23.1 %collective-permute-start.9 = (f32[8,896]{1,0:T(8,128)S(1)}, f32[8,896]{1,0:T(8,128)S(1)}, u32[]{:S(2)}, u32[]{:S(2)}) collective-permute-start(f32[8,896]{1,0:T(8,128)S(1)} %get-tuple-element.33.here), channel_id=1, source_target_pairs={{0,128},{16,144},{32,160},{48,176},{64,192},{80,208},{96,224},{112... | collective-permute-start | bytes 86024 | tf_op jit(solution)/shard_map/ppermute | solution.py:37
  42.0 10.5 %collective-permute-start.8 = (f32[8,896]{1,0:T(8,128)S(1)}, f32[8,896]{1,0:T(8,128)S(1)}, u32[]{:S(2)}, u32[]{:S(2)}) collective-permute-start(f32[8,896]{1,0:T(8,128)S(1)} %totals.3.here), channel_id=1, source_target_pairs={{0,128},{16,144},{32,160},{48,176},{64,192},{80,208},{96,224},{112... | collective-permute-start | bytes 86024 | tf_op jit(solution)/shard_map/ppermute | solution.py:37
  57.4 5.0 %collective-permute-start.10 = (bf16[896,256]{1,0:T(8,128)(2,1)S(1)}, bf16[896,256]{1,0:T(8,128)(2,1)S(1)}, u32[]{:S(2)}, u32[]{:S(2)}) collective-permute-start(bf16[896,256]{1,0:T(8,128)(2,1)S(1)} %get-tuple-element.43), channel_id=1, source_target_pairs={{0,16},{16,0},{32,48},{48,32},{64,80},{80,64},{96,112},{112,96},{1... | collective-permute-start | bytes 1376264 | tf_op jit(solution)/shard_map/ppermute | solution.py:33
  65.6 5.4 %collective-permute-start.13 = (bf16[448,256]{1,0:T(8,128)(2,1)S(1)}, bf16[448,256]{1,0:T(8,128)(2,1)S(1)}, u32[]{:S(2)}, u32[]{:S(2)}) collective-permute-start(bf16[448,256]{1,0:T(8,128)(2,1)S(1)} %get-tuple-element.49), channel_id=1, source_target_pairs={{0,16},{16,0},{32,48},{48,32},{64,80},{80,64},{96,112},{112,96},{1... | collective-permute-start | bytes 688136 | tf_op jit(solution)/shard_map/ppermute | solution.py:33
  66.2 14.7 %collective-permute-start.15 = (bf16[448,256]{1,0:T(8,128)(2,1)S(1)}, bf16[448,256]{1,0:T(8,128)(2,1)S(1)}, u32[]{:S(2)}, u32[]{:S(2)}) collective-permute-start(bf16[448,256]{1,0:T(8,128)(2,1)S(1)} %get-tuple-element.44), channel_id=1, source_target_pairs={{0,128},{16,144},{32,160},{48,176},{64,192},{80,208},{96,224},{112... | collective-permute-start | bytes 688136 | tf_op jit(solution)/shard_map/ppermute | solution.py:37
  69.3 11.6 %collective-permute-start.11 = (bf16[448,256]{1,0:T(8,128)(2,1)S(1)}, bf16[448,256]{1,0:T(8,128)(2,1)S(1)}, u32[]{:S(2)}, u32[]{:S(2)}) collective-permute-start(bf16[448,256]{1,0:T(8,128)(2,1)S(1)} %get-tuple-element.64), channel_id=1, source_target_pairs={{0,64},{16,80},{32,96},{48,112},{64,0},{80,16},{96,32},{112,48},{1... | collective-permute-start | bytes 688136 | tf_op jit(solution)/shard_map/ppermute | solution.py:29
  71.0 12.1 %collective-permute-start.12 = (bf16[448,256]{1,0:T(8,128)(2,1)S(1)}, bf16[448,256]{1,0:T(8,128)(2,1)S(1)}, u32[]{:S(2)}, u32[]{:S(2)}) collective-permute-start(bf16[448,256]{1,0:T(8,128)(2,1)S(1)} %get-tuple-element.63), channel_id=1, source_target_pairs={{0,32},{16,48},{32,64},{48,80},{64,96},{80,112},{96,0},{112,16},{1... | collective-permute-start | bytes 688136 | tf_op jit(solution)/shard_map/ppermute | solution.py:29
  71.1 12.0 %collective-permute-start.14 = (bf16[448,256]{1,0:T(8,128)(2,1)S(1)}, bf16[448,256]{1,0:T(8,128)(2,1)S(1)}, u32[]{:S(2)}, u32[]{:S(2)}) collective-permute-start(bf16[448,256]{1,0:T(8,128)(2,1)S(1)} %add_convert_fusion.1), channel_id=1, source_target_pairs={{0,96},{16,112},{32,0},{48,16},{64,32},{80,48},{96,64},{112,80},{1... | collective-permute-start | bytes 688136 | tf_op jit(solution)/shard_map/ppermute | solution.py:29
  77.7 5.4 %collective-permute-start.16 = (bf16[448,256]{1,0:T(8,128)(2,1)S(1)}, bf16[448,256]{1,0:T(8,128)(2,1)S(1)}, u32[]{:S(2)}, u32[]{:S(2)}) collective-permute-start(bf16[448,256]{1,0:T(8,128)(2,1)S(1)} %get-tuple-element.52), channel_id=1, source_target_pairs={{0,16},{16,0},{32,48},{48,32},{64,80},{80,64},{96,112},{112,96},{1... | collective-permute-start | bytes 688136 | tf_op jit(solution)/shard_map/ppermute | solution.py:33
  83.5 5.2 %collective-permute-start.17 = (bf16[448,128]{1,0:T(8,128)(2,1)S(1)}, bf16[448,128]{1,0:T(8,128)(2,1)S(1)}, u32[]{:S(2)}, u32[]{:S(2)}) collective-permute-start(bf16[448,128]{1,0:T(8,128)(2,1)S(1)} %pad_maximum_fusion.1), channel_id=1, source_target_pairs={{0,1},{1,0},{2,3},{3,2},{4,5},{5,4},{6,7},{7,6},{8,9},{9,8},{10,11... | collective-permute-start | bytes 344072 | tf_op jit(solution)/shard_map/ppermute | solution.py:41

commit v2 on v1

--- a/solution.py
+++ b/solution.py
@@ -178,10 +178,9 @@
 
 
 def far_kernel(places, qo_far, here, there, kv, *refs):
-    old, refs = (refs[0], refs[1:]) if len(refs) > 3 else (None, refs)
     out, *terms = refs
     rows = rows_of(qo_far, here, there)
-    total = None if old is None else old[...]
+    total = None
     for place, wide in zip(places, terms):
         term_k, term_v, term_q = tile(rows, kv.at[2 * place], kv.at[2 * place + 1])
         wide[:, :HD] = term_k
@@ -238,7 +237,7 @@
     wides, transposed = [((PAIR, 2 * HD), F32)] * 2, [((HD, LANES), F32)]
 
     def far_grads(places, *before):
-        outs = (halves[1:] if places[-1] == 0 else transposed) + wides
+        outs = (halves[1:] if places[-1] == 0 else transposed) + wides * 2
         return call(functools.partial(far_kernel, places), "far", outs, qo_far, there, here_far, kv, *before)
 
     def own_grads(places, *before):
@@ -249,17 +248,17 @@
     def joined(own_part, far_part):
         return (own_part + core_swapped(far_part).astype(F32)).astype(BF16)
 
-    dq_far, *terms = far_grads((3, 2))
-    *parts, dq = own_grads((3, 2), *terms)
-    dq_far, *terms = far_grads((1, 0), dq_far)
+    dq_far, *terms = far_grads((3, 2, 1, 0))
+    dq_there = far_swapped(dq_far)
+    terms[0], dq_far = lax.optimization_barrier((terms[0], dq_far))
+    *parts, dq = own_grads((3, 2), *terms[:2])
+    *part_c, dq = own_grads((1,), terms[2], dq)
     parts = joined(*parts)
     part_a, part_b = parts[:ROWS], parts[ROWS:]
     arrived = [turned(part_a, 2), turned(part_b, 1)]
-    dq_there = far_swapped(dq_far)
-    dq, part_a, part_b, dq_far = lax.optimization_barrier((dq, part_a, part_b, dq_far))
-    *parts, dq = own_grads((1,), terms[0], dq)
-    own_part, far_part, dq = own_grads((0,), terms[1], dq)
-    arrived.append(turned(joined(*parts), 3))
+    dq, part_a, part_b = lax.optimization_barrier((dq, part_a, part_b))
+    own_part, far_part, dq = own_grads((0,), terms[3], dq)
+    arrived.append(turned(joined(*part_c), 3))
     *arrived, dq_there = lax.optimization_barrier((*arrived, dq_there))
     grad = own_part + core_swapped(far_part).astype(F32)
     for part in arrived:

time: 89.6 us -> 88.4 us (0.987)
  starting transfers between devices: 34.5 us -> 29.4 us
  waiting for transfers between devices: 18.2 us -> 21.9 us
    ppermute x4, waiting for transfers between devices: 8.66 us -> 12.4 us  [far_swapped(): return lax.ppermute(block, 'ctx', [(i, i ^ 8) for i in range(16)])]
    ppermute x4, starting transfers between devices: 21.7 us -> 19 us  [far_swapped(): return lax.ppermute(block, 'ctx', [(i, i ^ 8) for i in range(16)])]
    ppermute x6, starting transfers between devices: 10.6 us -> 8.58 us  [turned(): return lax.ppermute(block, 'ctx', route)]
    pallas_call x8 -> x7, Pallas kernels: 32.1 us -> 32.2 us  [call(): pl.pallas_call(kernel, out_shape=[jax.ShapeDtypeStruct(*out) for out in o...]
  transfers between devices with their start and end apart: 18 -> 18, of which waited for: 6 -> 7; matrix products, arithmetic and copies ran while one was open for 2% -> 2% of each run, Pallas kernels for 26% -> 26%
where the time goes in v2:
time: 88.4 us; the launch traced here: 88.3 us
  Pallas kernels  32.2 us (36%)
  starting transfers between devices  29.4 us (33%)
  waiting for transfers between devices  21.9 us (25%)
  other arithmetic  2.57 us (3%)
  local copies, waits for them, and re-layouts  1.41 us (2%)
    pallas_call x7, Pallas kernels, call(): pl.pallas_call(kernel, out_shape=[jax.ShapeDtypeStruct(*out) for out in o...  32.2 us
    ppermute x4, starting transfers between devices, far_swapped(): return lax.ppermute(block, 'ctx', [(i, i ^ 8) for i in range(16)])  19 us
    ppermute x4, waiting for transfers between devices, far_swapped(): return lax.ppermute(block, 'ctx', [(i, i ^ 8) for i in range(16)])  12.4 us
    ppermute x6, starting transfers between devices, turned(): return lax.ppermute(block, 'ctx', route)  8.58 us
    ppermute x1, waiting for transfers between devices, pair_swapped(): return lax.ppermute(block, 'head', [(i, i ^ 1) for i in range(16)])  4.21 us
    ppermute x6, waiting for transfers between devices, turned(): return lax.ppermute(block, 'ctx', route)  3.12 us
    ppermute x7, waiting for transfers between devices, core_swapped(): return lax.ppermute(block, 'ctx', [(i, i ^ 1) for i in range(16)])  2.09 us
  transfers between devices with their start and end apart: 18, of which 7 were waited for; matrix products, arithmetic and copies ran while one was open for 2% of the time, Pallas kernels for 26%

profile of v2, /device:TPU:34, one launch (start us, length us, event | category | flops | bytes accessed | tf_op | source)
XLA Modules:
  0.0 88.3 jit_solution(6821859636170687832)
XLA Ops:
  0.6 0.7 convert_element_type.32
  1.4 1.0 %constant_dynamic-slice_fusion.2 = (bf16[448,128]{1,0:T(8,128)(2,1)S(1)}, bf16[448,128]{1,0:T(8,128)(2,1)S(1)}) fusion(bf16[448,1024]{1,0:T(8,128)(2,1)} %param.7, s32[]{:T(128)S(6)} %select_n.28, bf16[448,1024]{1,0:T(8,128)(2,1)} %param.6), kind=kLoop, calls=%fused_computation.11 | loop fusion | bytes 458756 | tf_op jit(solution)/shard_map/dynamic_slice | solution.py:222
  2.5 1.7 %collective-permute-start.2 = (bf16[464,256]{1,0:T(8,128)(2,1)S(1)}, bf16[464,256]{1,0:T(8,128)(2,1)S(1)}, u32[]{:S(2)}, u32[]{:S(2)}) collective-permute-start(bf16[464,256]{1,0:T(8,128)(2,1)S(1)} %maximum_maximum_fusion.1.refs_1_), channel_id=1, source_target_pairs={{0,32},{16,48},{32,64},{48,80},{64,96},{80,112},{96,0},{112,16},{1... | collective-permute-start | bytes 712712 | tf_op jit(solution)/shard_map/ppermute | solution.py:29
  4.2 1.7 %collective-permute-start.4 = (bf16[464,256]{1,0:T(8,128)(2,1)S(1)}, bf16[464,256]{1,0:T(8,128)(2,1)S(1)}, u32[]{:S(2)}, u32[]{:S(2)}) collective-permute-start(bf16[464,256]{1,0:T(8,128)(2,1)S(1)} %maximum_maximum_fusion.1.refs_1_), channel_id=1, source_target_pairs={{0,96},{16,112},{32,0},{48,16},{64,32},{80,48},{96,64},{112,80},{1... | collective-permute-start | bytes 712712 | tf_op jit(solution)/shard_map/ppermute | solution.py:29
  5.8 2.0 %collective-permute-start.6 = (bf16[464,256]{1,0:T(8,128)(2,1)S(1)}, bf16[464,256]{1,0:T(8,128)(2,1)S(1)}, u32[]{:S(2)}, u32[]{:S(2)}) collective-permute-start(bf16[464,256]{1,0:T(8,128)(2,1)S(1)} %maximum_maximum_fusion.1.refs_1_), channel_id=1, source_target_pairs={{0,64},{16,80},{32,96},{48,112},{64,0},{80,16},{96,32},{112,48},{1... | collective-permute-start | bytes 712712 | tf_op jit(solution)/shard_map/ppermute | solution.py:29
  7.8 1.2 %maximum_maximum_fusion.refs_0_.qo = bf16[464,512]{1,0:T(8,128)(2,1)S(1)} fusion(bf16[448,256]{1,0:T(8,128)(2,1)} %param.8, bf16[448,256]{1,0:T(8,128)(2,1)} %param.5, bf16[464]{0:T(512)(128)(2,1)S(1)} %pad.15.clone), kind=kLoop, calls=%fused_computation.1 | loop fusion | flops 1425408 | bytes 934816 | tf_op jit(solution)/shard_map/concatenate | solution.py:47
  9.0 6.4 %collective-permute-start = (bf16[464,512]{1,0:T(8,128)(2,1)S(1)}, bf16[464,512]{1,0:T(8,128)(2,1)S(1)}, u32[]{:S(2)}, u32[]{:S(2)}) collective-permute-start(bf16[464,512]{1,0:T(8,128)(2,1)S(1)} %maximum_maximum_fusion.refs_0_.qo), channel_id=1, source_target_pairs={{0,128},{16,144},{32,160},{48,176},{64,192},{80,208},{96,224},{112... | collective-permute-start | bytes 1425416 | tf_op jit(solution)/shard_map/ppermute | solution.py:37
  16.0 1.6 %collective-permute-done.6.refs_7_ = bf16[464,256]{1,0:T(8,128)(2,1)S(1)} collective-permute-done((bf16[464,256]{1,0:T(8,128)(2,1)S(1)}, bf16[464,256]{1,0:T(8,128)(2,1)S(1)}, u32[]{:S(2)}, u32[]{:S(2)}) %collective-permute-start.6) | collective-permute-done | bytes 237600 | tf_op jit(solution)/shard_map/ppermute | solution.py:29
  17.7 1.5 %collective-permute-done.7.refs_8_ = bf16[464,256]{1,0:T(8,128)(2,1)S(1)} collective-permute-done((bf16[464,256]{1,0:T(8,128)(2,1)S(1)}, bf16[464,256]{1,0:T(8,128)(2,1)S(1)}, u32[]{:S(2)}, u32[]{:S(2)}) %collective-permute-start.7) | collective-permute-done | bytes 237600 | tf_op jit(solution)/shard_map/ppermute | solution.py:33
  19.1 5.5 %totals.2 = (f32[8,896]{1,0:T(8,128)S(1)}, bf16[8,464,256]{2,1,0:T(8,128)(2,1)S(1)}) custom-call(bf16[464,512]{1,0:T(8,128)(2,1)S(1)} %maximum_maximum_fusion.refs_0_.qo, bf16[464,256]{1,0:T(8,128)(2,1)S(1)} %maximum_maximum_fusion.1.refs_1_, bf16[464,256]{1,0:T(8,128)(2,1)S(1)} %collective-permute-done.1.refs_2_, ...), custom_call_target="tpu_custom_call" | custom-call | flops 1048576 | bytes 65536 | tf_op jit(solution)/shard_map/totals/pallas_call | solution.py:122
  24.7 6.4 %collective-permute-start.9 = (f32[8,896]{1,0:T(8,128)S(1)}, f32[8,896]{1,0:T(8,128)S(1)}, u32[]{:S(2)}, u32[]{:S(2)}) collective-permute-start(f32[8,896]{1,0:T(8,128)S(1)} %get-tuple-element.33.here), channel_id=1, source_target_pairs={{0,128},{16,144},{32,160},{48,176},{64,192},{80,208},{96,224},{112... | collective-permute-start | bytes 86024 | tf_op jit(solution)/shard_map/ppermute | solution.py:37
  31.1 5.5 %collective-permute-done.refs_0_.qo_far = bf16[464,512]{1,0:T(8,128)(2,1)S(1)} collective-permute-done((bf16[464,512]{1,0:T(8,128)(2,1)S(1)}, bf16[464,512]{1,0:T(8,128)(2,1)S(1)}, u32[]{:S(2)}, u32[]{:S(2)}) %collective-permute-start) | collective-permute-done | bytes 475168 | tf_op jit(solution)/shard_map/ppermute | solution.py:37
  36.6 5.4 %totals.3.here = f32[8,896]{1,0:T(8,128)S(1)} custom-call(bf16[464,512]{1,0:T(8,128)(2,1)S(1)} %collective-permute-done.refs_0_.qo_far, bf16[8,464,256]{2,1,0:T(8,128)(2,1)S(1)} %get-tuple-element.35.refs_1_.kv), custom_call_target="tpu_custom_call" | custom-call | flops 1048576 | bytes 65536 | tf_op jit(solution)/shard_map/totals/pallas_call | solution.py:122
  42.0 5.8 %collective-permute-start.8 = (f32[8,896]{1,0:T(8,128)S(1)}, f32[8,896]{1,0:T(8,128)S(1)}, u32[]{:S(2)}, u32[]{:S(2)}) collective-permute-start(f32[8,896]{1,0:T(8,128)S(1)} %totals.3.here), channel_id=1, source_target_pairs={{0,128},{16,144},{32,160},{48,176},{64,192},{80,208},{96,224},{112... | collective-permute-start | bytes 86024 | tf_op jit(solution)/shard_map/ppermute | solution.py:37
  47.8 9.2 %far.1 = (bf16[448,256]{1,0:T(8,128)(2,1)S(1)}, f32[896,256]{1,0:T(8,128)S(1)}, f32[896,256]{1,0:T(8,128)S(1)}, f32[896,256]{1,0:T(8,128)S(1)}, f32[896,256]{1,0:T(8,128)S(1)}) custom-call(bf16[464,512]{1,0:T(8,128)(2,1)S(1)} %collective-permute-done.refs_0_.qo_far, f32[8,896]{1,0:T(8,128)S(1)} %totals.3.here, f32[8,896]{1,0:T(8,128)S(1)} %collective-permute-done.9.there, ...), custom_call_target="tpu_custom_call" | custom-call | flops 1048576 | bytes 65536 | tf_op jit(solution)/shard_map/far/pallas_call | solution.py:122
  57.1 5.2 %own.3 = (f32[896,256]{1,0:T(8,128)S(1)}, bf16[896,256]{1,0:T(8,128)(2,1)S(1)}, f32[128,896]{1,0:T(8,128)S(1)}) custom-call(bf16[464,512]{1,0:T(8,128)(2,1)S(1)} %maximum_maximum_fusion.refs_0_.qo, f32[8,896]{1,0:T(8,128)S(1)} %get-tuple-element.33.here, f32[8,896]{1,0:T(8,128)S(1)} %collective-permute-done.8.there, ...), custom_call_target="tpu_custom_call" | custom-call | flops 1048576 | bytes 65536 | tf_op jit(solution)/shard_map/own/pallas_call | solution.py:122
  62.3 3.0 %own.4 = (f32[448,256]{1,0:T(8,128)S(1)}, bf16[448,256]{1,0:T(8,128)(2,1)S(1)}, f32[128,896]{1,0:T(8,128)S(1)}) custom-call(bf16[464,512]{1,0:T(8,128)(2,1)S(1)} %maximum_maximum_fusion.refs_0_.qo, f32[8,896]{1,0:T(8,128)S(1)} %get-tuple-element.33.here, f32[8,896]{1,0:T(8,128)S(1)} %collective-permute-done.8.there, ...), custom_call_target="tpu_custom_call" | custom-call | flops 1048576 | bytes 65536 | tf_op jit(solution)/shard_map/own/pallas_call | solution.py:122
  66.9 0.9 collective-permute-start.14
  67.9 2.1 %collective-permute-start.11 = (bf16[448,256]{1,0:T(8,128)(2,1)S(1)}, bf16[448,256]{1,0:T(8,128)(2,1)S(1)}, u32[]{:S(2)}, u32[]{:S(2)}) collective-permute-start(bf16[448,256]{1,0:T(8,128)(2,1)S(1)} %get-tuple-element.64), channel_id=1, source_target_pairs={{0,64},{16,80},{32,96},{48,112},{64,0},{80,16},{96,32},{112,48},{1... | collective-permute-start | bytes 688136 | tf_op jit(solution)/shard_map/ppermute | solution.py:29
  70.4 3.0 %own.5 = (f32[448,256]{1,0:T(8,128)S(1)}, bf16[448,256]{1,0:T(8,128)(2,1)S(1)}, f32[448,256]{1,0:T(8,128)S(1)}) custom-call(bf16[464,512]{1,0:T(8,128)(2,1)S(1)} %maximum_maximum_fusion.refs_0_.qo, f32[8,896]{1,0:T(8,128)S(1)} %get-tuple-element.33.here, f32[8,896]{1,0:T(8,128)S(1)} %collective-permute-done.8.there, ...), custom_call_target="tpu_custom_call" | custom-call | flops 1048576 | bytes 65536 | tf_op jit(solution)/shard_map/own/pallas_call | solution.py:122
  73.5 6.9 %collective-permute-done.15.dq_far = bf16[448,256]{1,0:T(8,128)(2,1)S(1)} collective-permute-done((bf16[448,256]{1,0:T(8,128)(2,1)S(1)}, bf16[448,256]{1,0:T(8,128)(2,1)S(1)}, u32[]{:S(2)}, u32[]{:S(2)}) %collective-permute-start.15) | collective-permute-done | bytes 229408 | tf_op jit(solution)/shard_map/ppermute | solution.py:37
  80.4 1.5 %collective-permute-done.12 = bf16[448,256]{1,0:T(8,128)(2,1)S(1)} collective-permute-done((bf16[448,256]{1,0:T(8,128)(2,1)S(1)}, bf16[448,256]{1,0:T(8,128)(2,1)S(1)}, u32[]{:S(2)}, u32[]{:S(2)}) %collective-permute-start.12) | collective-permute-done | bytes 229408 | tf_op jit(solution)/shard_map/ppermute | solution.py:29
  83.2 4.2 %collective-permute-done.17.incoming = bf16[448,128]{1,0:T(8,128)(2,1)S(1)} collective-permute-done((bf16[448,128]{1,0:T(8,128)(2,1)S(1)}, bf16[448,128]{1,0:T(8,128)(2,1)S(1)}, u32[]{:S(2)}, u32[]{:S(2)}) %collective-permute-start.17) | collective-permute-done | bytes 114720 | tf_op jit(solution)/shard_map/ppermute | solution.py:41
  87.4 0.9 finish.1
  (33 shorter events, 4.4 us)
Async XLA Ops:
  2.5 12.9 %collective-permute-start.2 = (bf16[464,256]{1,0:T(8,128)(2,1)S(1)}, bf16[464,256]{1,0:T(8,128)(2,1)S(1)}, u32[]{:S(2)}, u32[]{:S(2)}) collective-permute-start(bf16[464,256]{1,0:T(8,128)(2,1)S(1)} %maximum_maximum_fusion.1.refs_1_), channel_id=1, source_target_pairs={{0,32},{16,48},{32,64},{48,80},{64,96},{80,112},{96,0},{112,16},{1... | collective-permute-start | bytes 712712 | tf_op jit(solution)/shard_map/ppermute | solution.py:29
  4.2 11.7 %collective-permute-start.4 = (bf16[464,256]{1,0:T(8,128)(2,1)S(1)}, bf16[464,256]{1,0:T(8,128)(2,1)S(1)}, u32[]{:S(2)}, u32[]{:S(2)}) collective-permute-start(bf16[464,256]{1,0:T(8,128)(2,1)S(1)} %maximum_maximum_fusion.1.refs_1_), channel_id=1, source_target_pairs={{0,96},{16,112},{32,0},{48,16},{64,32},{80,48},{96,64},{112,80},{1... | collective-permute-start | bytes 712712 | tf_op jit(solution)/shard_map/ppermute | solution.py:29
  5.8 11.8 %collective-permute-start.6 = (bf16[464,256]{1,0:T(8,128)(2,1)S(1)}, bf16[464,256]{1,0:T(8,128)(2,1)S(1)}, u32[]{:S(2)}, u32[]{:S(2)}) collective-permute-start(bf16[464,256]{1,0:T(8,128)(2,1)S(1)} %maximum_maximum_fusion.1.refs_1_), channel_id=1, source_target_pairs={{0,64},{16,80},{32,96},{48,112},{64,0},{80,16},{96,32},{112,48},{1... | collective-permute-start | bytes 712712 | tf_op jit(solution)/shard_map/ppermute | solution.py:29
  9.0 27.6 %collective-permute-start = (bf16[464,512]{1,0:T(8,128)(2,1)S(1)}, bf16[464,512]{1,0:T(8,128)(2,1)S(1)}, u32[]{:S(2)}, u32[]{:S(2)}) collective-permute-start(bf16[464,512]{1,0:T(8,128)(2,1)S(1)} %maximum_maximum_fusion.refs_0_.qo), channel_id=1, source_target_pairs={{0,128},{16,144},{32,160},{48,176},{64,192},{80,208},{96,224},{112... | collective-permute-start | bytes 1425416 | tf_op jit(solution)/shard_map/ppermute | solution.py:37
  15.4 2.3 %collective-permute-start.1 = (bf16[464,256]{1,0:T(8,128)(2,1)S(1)}, bf16[464,256]{1,0:T(8,128)(2,1)S(1)}, u32[]{:S(2)}, u32[]{:S(2)}) collective-permute-start(bf16[464,256]{1,0:T(8,128)(2,1)S(1)} %maximum_maximum_fusion.1.refs_1_), channel_id=1, source_target_pairs={{0,16},{16,0},{32,48},{48,32},{64,80},{80,64},{96,112},{112,96},{1... | collective-permute-start | bytes 712712 | tf_op jit(solution)/shard_map/ppermute | solution.py:33
  15.4 2.3 %collective-permute-start.3 = (bf16[464,256]{1,0:T(8,128)(2,1)S(1)}, bf16[464,256]{1,0:T(8,128)(2,1)S(1)}, u32[]{:S(2)}, u32[]{:S(2)}) collective-permute-start(bf16[464,256]{1,0:T(8,128)(2,1)S(1)} %collective-permute-done.2.refs_3_), channel_id=1, source_target_pairs={{0,16},{16,0},{32,48},{48,32},{64,80},{80,64},{96,112},{112,96},{1... | collective-permute-start | bytes 712712 | tf_op jit(solution)/shard_map/ppermute | solution.py:33
  15.9 1.8 %collective-permute-start.5 = (bf16[464,256]{1,0:T(8,128)(2,1)S(1)}, bf16[464,256]{1,0:T(8,128)(2,1)S(1)}, u32[]{:S(2)}, u32[]{:S(2)}) collective-permute-start(bf16[464,256]{1,0:T(8,128)(2,1)S(1)} %collective-permute-done.4.refs_5_), channel_id=1, source_target_pairs={{0,16},{16,0},{32,48},{48,32},{64,80},{80,64},{96,112},{112,96},{1... | collective-permute-start | bytes 712712 | tf_op jit(solution)/shard_map/ppermute | solution.py:33
  17.6 1.5 %collective-permute-start.7 = (bf16[464,256]{1,0:T(8,128)(2,1)S(1)}, bf16[464,256]{1,0:T(8,128)(2,1)S(1)}, u32[]{:S(2)}, u32[]{:S(2)}) collective-permute-start(bf16[464,256]{1,0:T(8,128)(2,1)S(1)} %collective-permute-done.6.refs_7_), channel_id=1, source_target_pairs={{0,16},{16,0},{32,48},{48,32},{64,80},{80,64},{96,112},{112,96},{1... | collective-permute-start | bytes 712712 | tf_op jit(solution)/shard_map/ppermute | solution.py:33
  24.7 23.1 %collective-permute-start.9 = (f32[8,896]{1,0:T(8,128)S(1)}, f32[8,896]{1,0:T(8,128)S(1)}, u32[]{:S(2)}, u32[]{:S(2)}) collective-permute-start(f32[8,896]{1,0:T(8,128)S(1)} %get-tuple-element.33.here), channel_id=1, source_target_pairs={{0,128},{16,144},{32,160},{48,176},{64,192},{80,208},{96,224},{112... | collective-permute-start | bytes 86024 | tf_op jit(solution)/shard_map/ppermute | solution.py:37
  42.0 15.1 %collective-permute-start.8 = (f32[8,896]{1,0:T(8,128)S(1)}, f32[8,896]{1,0:T(8,128)S(1)}, u32[]{:S(2)}, u32[]{:S(2)}) collective-permute-start(f32[8,896]{1,0:T(8,128)S(1)} %totals.3.here), channel_id=1, source_target_pairs={{0,128},{16,144},{32,160},{48,176},{64,192},{80,208},{96,224},{112... | collective-permute-start | bytes 86024 | tf_op jit(solution)/shard_map/ppermute | solution.py:37
  65.2 1.6 %collective-permute-start.13 = (bf16[448,256]{1,0:T(8,128)(2,1)S(1)}, bf16[448,256]{1,0:T(8,128)(2,1)S(1)}, u32[]{:S(2)}, u32[]{:S(2)}) collective-permute-start(bf16[448,256]{1,0:T(8,128)(2,1)S(1)} %get-tuple-element.49), channel_id=1, source_target_pairs={{0,16},{16,0},{32,48},{48,32},{64,80},{80,64},{96,112},{112,96},{1... | collective-permute-start | bytes 688136 | tf_op jit(solution)/shard_map/ppermute | solution.py:33
  65.3 2.4 %collective-permute-start.10 = (bf16[896,256]{1,0:T(8,128)(2,1)S(1)}, bf16[896,256]{1,0:T(8,128)(2,1)S(1)}, u32[]{:S(2)}, u32[]{:S(2)}) collective-permute-start(bf16[896,256]{1,0:T(8,128)(2,1)S(1)} %get-tuple-element.45), channel_id=1, source_target_pairs={{0,16},{16,0},{32,48},{48,32},{64,80},{80,64},{96,112},{112,96},{1... | collective-permute-start | bytes 1376264 | tf_op jit(solution)/shard_map/ppermute | solution.py:33
  65.8 14.6 %collective-permute-start.15 = (bf16[448,256]{1,0:T(8,128)(2,1)S(1)}, bf16[448,256]{1,0:T(8,128)(2,1)S(1)}, u32[]{:S(2)}, u32[]{:S(2)}) collective-permute-start(bf16[448,256]{1,0:T(8,128)(2,1)S(1)} %get-tuple-element.39), channel_id=1, source_target_pairs={{0,128},{16,144},{32,160},{48,176},{64,192},{80,208},{96,224},{112... | collective-permute-start | bytes 688136 | tf_op jit(solution)/shard_map/ppermute | solution.py:37
  66.9 13.5 %collective-permute-start.14 = (bf16[448,256]{1,0:T(8,128)(2,1)S(1)}, bf16[448,256]{1,0:T(8,128)(2,1)S(1)}, u32[]{:S(2)}, u32[]{:S(2)}) collective-permute-start(bf16[448,256]{1,0:T(8,128)(2,1)S(1)} %add_convert_fusion.1), channel_id=1, source_target_pairs={{0,96},{16,112},{32,0},{48,16},{64,32},{80,48},{96,64},{112,80},{1... | collective-permute-start | bytes 688136 | tf_op jit(solution)/shard_map/ppermute | solution.py:29
  67.9 12.5 %collective-permute-start.11 = (bf16[448,256]{1,0:T(8,128)(2,1)S(1)}, bf16[448,256]{1,0:T(8,128)(2,1)S(1)}, u32[]{:S(2)}, u32[]{:S(2)}) collective-permute-start(bf16[448,256]{1,0:T(8,128)(2,1)S(1)} %get-tuple-element.64), channel_id=1, source_target_pairs={{0,64},{16,80},{32,96},{48,112},{64,0},{80,16},{96,32},{112,48},{1... | collective-permute-start | bytes 688136 | tf_op jit(solution)/shard_map/ppermute | solution.py:29
  70.0 11.9 %collective-permute-start.12 = (bf16[448,256]{1,0:T(8,128)(2,1)S(1)}, bf16[448,256]{1,0:T(8,128)(2,1)S(1)}, u32[]{:S(2)}, u32[]{:S(2)}) collective-permute-start(bf16[448,256]{1,0:T(8,128)(2,1)S(1)} %get-tuple-element.63), channel_id=1, source_target_pairs={{0,32},{16,48},{32,64},{48,80},{64,96},{80,112},{96,0},{112,16},{1... | collective-permute-start | bytes 688136 | tf_op jit(solution)/shard_map/ppermute | solution.py:29
  73.3 8.5 %collective-permute-start.16 = (bf16[448,256]{1,0:T(8,128)(2,1)S(1)}, bf16[448,256]{1,0:T(8,128)(2,1)S(1)}, u32[]{:S(2)}, u32[]{:S(2)}) collective-permute-start(bf16[448,256]{1,0:T(8,128)(2,1)S(1)} %get-tuple-element.52), channel_id=1, source_target_pairs={{0,16},{16,0},{32,48},{48,32},{64,80},{80,64},{96,112},{112,96},{1... | collective-permute-start | bytes 688136 | tf_op jit(solution)/shard_map/ppermute | solution.py:33
  82.3 5.2 %collective-permute-start.17 = (bf16[448,128]{1,0:T(8,128)(2,1)S(1)}, bf16[448,128]{1,0:T(8,128)(2,1)S(1)}, u32[]{:S(2)}, u32[]{:S(2)}) collective-permute-start(bf16[448,128]{1,0:T(8,128)(2,1)S(1)} %pad_maximum_fusion.1), channel_id=1, source_target_pairs={{0,1},{1,0},{2,3},{3,2},{4,5},{5,4},{6,7},{7,6},{8,9},{9,8},{10,11... | collective-permute-start | bytes 344072 | tf_op jit(solution)/shard_map/ppermute | solution.py:41
